TPU v7x, 32 devices: a whole 2x2x4 slice. The times are simulated.
32 devices in a mesh: dp: 4 (over y, x), fsdp: 4 (over z), ctx: 2 (over core).
Axes of the slice: x: 2, y: 2, z: 4, core: 2. Of those that a mesh axis runs over, the one named last changes fastest.
Arguments:
- inputs: bfloat16 [16, 1024, 768], P(('dp', 'fsdp'), 'ctx'), may hold values from -6 to 6
- cotangent: bfloat16 [16, 1024, 768], P(('dp', 'fsdp'), 'ctx'), may hold values from -6 to 6
- slot_order: int32 [4], replicated, may hold values from 0 to 3, each once
- w_qkv: bfloat16 [768, 2304], P('fsdp'), may hold values from -0.3125 to 0.3125
- w_out: bfloat16 [768, 768], P('fsdp'), may hold values from -0.875 to 0.875
- w_up: bfloat16 [768, 3072], P('fsdp'), may hold values from -0.21875 to 0.21875
- w_down: bfloat16 [3072, 768], P('fsdp'), may hold values from -0.109375 to 0.109375
- qv_bias: bfloat16 [2, 768], P(None, 'fsdp'), may hold values from -2 to 2
- out_bias: bfloat16 [768], P('fsdp'), may hold values from -2 to 2
- up_bias: bfloat16 [3072], P('fsdp'), may hold values from -3 to 3
- down_bias: bfloat16 [768], P('fsdp'), may hold values from -2 to 2
- norm1_gain: bfloat16 [768], P('fsdp'), may hold values from 0.5 to 1.5
- norm1_shift: bfloat16 [768], P('fsdp'), may hold values from -2 to 2
- norm2_gain: bfloat16 [768], P('fsdp'), may hold values from 0.5 to 1.5
- norm2_shift: bfloat16 [768], P('fsdp'), may hold values from -2 to 2
Outputs:
- outputs: bfloat16 [16, 1024, 768], P(('dp', 'fsdp'), 'ctx')
- input_grad: bfloat16 [16, 1024, 768], P(('dp', 'fsdp'), 'ctx')
- grad_w_qkv: float32 [768, 2304], P('fsdp')
- grad_w_out: float32 [768, 768], P('fsdp')
- grad_w_up: float32 [768, 3072], P('fsdp')
- grad_w_down: float32 [3072, 768], P('fsdp')
- grad_qv_bias: float32 [2, 768], P(None, 'fsdp')
- grad_out_bias: float32 [768], P('fsdp')
- grad_up_bias: float32 [3072], P('fsdp')
- grad_down_bias: float32 [768], P('fsdp')
- grad_norm1_gain: float32 [768], P('fsdp')
- grad_norm1_shift: float32 [768], P('fsdp')
- grad_norm2_gain: float32 [768], P('fsdp')
- grad_norm2_shift: float32 [768], P('fsdp')
Inputs may be any that keep to these rules, and one draw needn't show every extreme that they name: Each position block number appears once; storage slot b of every sequence holds positions slot_order[b] * 256 to slot_order[b] * 256 + 255.
All inputs are finite; a program needn't handle non-finite values.
Results may differ from a plain program's by a relative error of at most 0.018.
Values may be sent and summed in bfloat16 or wider, within the bound.
A program may use at most 192 MiB of HBM per device.

v0:
```python
import math

import jax
import jax.numpy as jnp
from jax import lax
from jax.sharding import PartitionSpec as P

HEADS = 12
HD = 64


EPSILON = 1e-05
MASKED = -1e30
GELU_COEF = 0.7978845608028654


def gelu_tanh(pre_act):
    return (
        0.5
        * pre_act
        * (1.0 + jnp.tanh(GELU_COEF * (pre_act + 0.044715 * pre_act * pre_act * pre_act)))
    )


def normalize(rows_in):
    row_mean = jnp.mean(rows_in, axis=-1, keepdims=True)
    centered = rows_in - row_mean
    variance = jnp.mean(centered * centered, axis=-1, keepdims=True)
    row_scale = lax.rsqrt(variance + EPSILON)
    return (centered * row_scale, row_scale)


def norm_back(grad_out, normed, row_scale, gain_vec):
    shaped = grad_out * gain_vec
    return row_scale * (
        shaped
        - jnp.mean(shaped, axis=-1, keepdims=True)
        - normed * jnp.mean(shaped * normed, axis=-1, keepdims=True)
    )


def token_places(slot_ids, slot_order, piece_len):
    slot_block = slot_ids // piece_len
    block_ids = jnp.arange(slot_order.shape[0], dtype=jnp.int32)
    matches = (slot_block[:, None] == block_ids[None, :]).astype(jnp.int32)
    return jnp.sum(matches * slot_order[None, :], axis=1) * piece_len + slot_ids % piece_len


def attend_piece(state_now, piece_pair, queries, query_places, slot_order, piece_len, scaling):
    key_piece, value_piece = piece_pair
    seq_count = key_piece.shape[0]
    key_count = key_piece.shape[1]
    block_width = math.gcd(key_count, 512)
    block_count = key_count // block_width

    def one_block(block_index, carried):
        row_max, row_total, weighted = carried
        offset = block_index * block_width
        key_block = lax.dynamic_slice_in_dim(key_piece, offset, block_width, 1).reshape(
            seq_count, block_width, HEADS, HD
        )
        value_block = lax.dynamic_slice_in_dim(value_piece, offset, block_width, 1).reshape(
            seq_count, block_width, HEADS, HD
        )
        key_places = token_places(
            offset + jnp.arange(block_width, dtype=jnp.int32), slot_order, piece_len
        )
        scores = (
            jnp.einsum("sqhd,skhd->sqhk", queries, key_block, preferred_element_type=jnp.float32)
            * scaling
        )
        allowed = key_places[None, None, None, :] <= query_places[None, :, None, None]
        scores = jnp.where(allowed, scores, MASKED)
        new_max = jnp.maximum(row_max, jnp.max(scores, axis=-1))
        weights = jnp.where(allowed, jnp.exp(scores - new_max[..., None]), 0.0)
        factor = jnp.exp(row_max - new_max)
        row_total = row_total * factor + jnp.sum(weights, axis=-1)
        weighted = weighted * factor[..., None] + jnp.einsum(
            "sqhk,skhd->sqhd",
            weights.astype(jnp.bfloat16),
            value_block,
            preferred_element_type=jnp.float32,
        )
        return (new_max, row_total, weighted)

    return lax.fori_loop(0, block_count, one_block, state_now)


def body(
    inputs,
    cotangent,
    slot_order,
    w_qkv,
    w_out,
    w_up,
    w_down,
    qv_bias,
    out_bias,
    up_bias,
    down_bias,
    norm1_gain,
    norm1_shift,
    norm2_gain,
    norm2_shift,
):
    seq_count, local_len, model_width = inputs.shape
    row_count = seq_count * local_len
    piece_len = local_len // 2
    scaling = HD ** (-0.5)
    gathered_weights = (
        lax.all_gather(w_qkv, "fsdp", axis=0, tiled=True),
        lax.all_gather(w_out, "fsdp", axis=0, tiled=True),
        lax.all_gather(w_up, "fsdp", axis=0, tiled=True),
        lax.all_gather(w_down, "fsdp", axis=0, tiled=True),
        lax.all_gather(qv_bias, "fsdp", axis=1, tiled=True),
        lax.all_gather(out_bias, "fsdp", axis=0, tiled=True),
        lax.all_gather(up_bias, "fsdp", axis=0, tiled=True),
        lax.all_gather(down_bias, "fsdp", axis=0, tiled=True),
        lax.all_gather(norm1_gain, "fsdp", axis=0, tiled=True),
        lax.all_gather(norm1_shift, "fsdp", axis=0, tiled=True),
        lax.all_gather(norm2_gain, "fsdp", axis=0, tiled=True),
        lax.all_gather(norm2_shift, "fsdp", axis=0, tiled=True),
    )
    (
        whole_qkv,
        whole_out,
        whole_up,
        whole_down,
        whole_qv,
        whole_ob,
        whole_ub,
        whole_db,
        gain_one,
        shift_one,
        gain_two,
        shift_two,
    ) = gathered_weights
    flat_in = inputs.reshape(row_count, model_width).astype(jnp.float32)
    normed_one, scale_one = normalize(flat_in)
    hidden_one = (normed_one * gain_one.astype(jnp.float32) + shift_one.astype(jnp.float32)).astype(
        jnp.bfloat16
    )
    projected = jnp.dot(hidden_one, whole_qkv, preferred_element_type=jnp.float32)
    bias_rows = whole_qv.astype(jnp.float32)
    queries = (
        (projected[:, :model_width] + bias_rows[0])
        .astype(jnp.bfloat16)
        .reshape(seq_count, local_len, HEADS, HD)
    )
    key_rows = (
        projected[:, model_width : 2 * model_width]
        .astype(jnp.bfloat16)
        .reshape(seq_count, local_len, model_width)
    )
    value_rows = (
        (projected[:, 2 * model_width :] + bias_rows[1])
        .astype(jnp.bfloat16)
        .reshape(seq_count, local_len, model_width)
    )
    slot_ids = lax.axis_index("ctx") * local_len + jnp.arange(local_len, dtype=jnp.int32)
    query_places = token_places(slot_ids, slot_order, piece_len)
    start_state = (
        jnp.full((seq_count, local_len, HEADS), MASKED, jnp.float32),
        jnp.zeros((seq_count, local_len, HEADS), jnp.float32),
        jnp.zeros((seq_count, local_len, HEADS, HD), jnp.float32),
    )
    final_state = attend_piece(
        start_state,
        (
            lax.all_gather(key_rows, "ctx", axis=1, tiled=True),
            lax.all_gather(value_rows, "ctx", axis=1, tiled=True),
        ),
        queries,
        query_places,
        slot_order,
        piece_len,
        scaling,
    )
    row_max, row_total, weighted = final_state
    attended_f32 = weighted / row_total[..., None]
    log_total = row_max + jnp.log(row_total)
    attended = attended_f32.reshape(row_count, model_width).astype(jnp.bfloat16)
    middle = (
        flat_in
        + jnp.dot(attended, whole_out, preferred_element_type=jnp.float32)
        + whole_ob.astype(jnp.float32)
    )
    normed_two, scale_two = normalize(middle)
    hidden_two = (normed_two * gain_two.astype(jnp.float32) + shift_two.astype(jnp.float32)).astype(
        jnp.bfloat16
    )
    pre_act = jnp.dot(hidden_two, whole_up, preferred_element_type=jnp.float32) + whole_ub.astype(
        jnp.float32
    )
    activated = gelu_tanh(pre_act).astype(jnp.bfloat16)
    result = (
        middle
        + jnp.dot(activated, whole_down, preferred_element_type=jnp.float32)
        + whole_db.astype(jnp.float32)
    )
    outputs = result.astype(jnp.bfloat16).reshape(seq_count, local_len, model_width)
    whole_qkv, whole_out, whole_up, whole_down, gain_one, gain_two = (
        lax.all_gather(w_qkv, "fsdp", axis=0, tiled=True),
        lax.all_gather(w_out, "fsdp", axis=0, tiled=True),
        lax.all_gather(w_up, "fsdp", axis=0, tiled=True),
        lax.all_gather(w_down, "fsdp", axis=0, tiled=True),
        lax.all_gather(norm1_gain, "fsdp", axis=0, tiled=True),
        lax.all_gather(norm2_gain, "fsdp", axis=0, tiled=True),
    )
    grad_rows = cotangent.reshape(row_count, model_width)
    grad_rows_f32 = grad_rows.astype(jnp.float32)
    grad_down = jnp.einsum("rf,rd->fd", activated, grad_rows, preferred_element_type=jnp.float32)
    grad_down_bias = jnp.sum(grad_rows_f32, axis=0)
    grad_act = jnp.einsum("rd,fd->rf", grad_rows, whole_down, preferred_element_type=jnp.float32)
    gelu_value, gelu_pull = jax.vjp(gelu_tanh, pre_act)
    grad_pre = gelu_pull(grad_act)[0].astype(jnp.bfloat16)
    grad_up = jnp.einsum("rd,rf->df", hidden_two, grad_pre, preferred_element_type=jnp.float32)
    grad_up_bias = jnp.sum(grad_pre.astype(jnp.float32), axis=0)
    grad_hidden_two = jnp.einsum(
        "rf,df->rd", grad_pre, whole_up, preferred_element_type=jnp.float32
    )
    grad_gain_two = jnp.sum(grad_hidden_two * normed_two, axis=0)
    grad_shift_two = jnp.sum(grad_hidden_two, axis=0)
    grad_middle = grad_rows_f32 + norm_back(
        grad_hidden_two, normed_two, scale_two, gain_two.astype(jnp.float32)
    )
    grad_branch = grad_middle.astype(jnp.bfloat16)
    grad_out = jnp.einsum("rd,re->de", attended, grad_branch, preferred_element_type=jnp.float32)
    grad_out_bias = jnp.sum(grad_branch.astype(jnp.float32), axis=0)
    grad_attended = (
        jnp.einsum("re,de->rd", grad_branch, whole_out, preferred_element_type=jnp.float32)
        .astype(jnp.bfloat16)
        .reshape(seq_count, local_len, HEADS, HD)
    )
    row_delta = jnp.sum(grad_attended.astype(jnp.float32) * attended_f32, axis=-1)
    gathered = (
        lax.all_gather(key_rows, "ctx", axis=1, tiled=True),
        lax.all_gather(value_rows, "ctx", axis=1, tiled=True),
    )
    gathered_keys, gathered_values = gathered
    key_count = gathered_keys.shape[1]
    block_width = math.gcd(local_len, 512)
    block_count = key_count // block_width

    def score_grads(
        query_block,
        grad_block,
        total_block,
        delta_block,
        block_places,
        key_block,
        value_block,
        key_places,
    ):
        allowed = key_places[None, None, None, :] <= block_places[None, :, None, None]
        scores = (
            jnp.einsum(
                "sqhd,skhd->sqhk", query_block, key_block, preferred_element_type=jnp.float32
            )
            * scaling
        )
        soft_probs = jnp.where(
            allowed, jnp.exp(jnp.where(allowed, scores - total_block[..., None], 0.0)), 0.0
        )
        grad_probs = jnp.einsum(
            "sqhd,skhd->sqhk", grad_block, value_block, preferred_element_type=jnp.float32
        )
        grad_scores = (soft_probs * (grad_probs - delta_block[..., None])).astype(jnp.bfloat16)
        return (soft_probs, grad_scores)

    def remote_block(offset):
        key_block = lax.dynamic_slice_in_dim(gathered_keys, offset, block_width, 1).reshape(
            seq_count, block_width, HEADS, HD
        )
        value_block = lax.dynamic_slice_in_dim(gathered_values, offset, block_width, 1).reshape(
            seq_count, block_width, HEADS, HD
        )
        key_places = token_places(
            offset + jnp.arange(block_width, dtype=jnp.int32), slot_order, piece_len
        )
        soft_probs, grad_scores = score_grads(
            queries,
            grad_attended,
            log_total,
            row_delta,
            query_places,
            key_block,
            value_block,
            key_places,
        )
        return (key_block, soft_probs, grad_scores)

    zero_queries = jnp.zeros((seq_count, local_len, HEADS, HD), jnp.float32)

    def back_block(grad_queries, block_index):
        key_block, soft_probs, grad_scores = remote_block(block_index * block_width)
        grad_queries = (
            grad_queries
            + jnp.einsum(
                "sqhk,skhd->sqhd", grad_scores, key_block, preferred_element_type=jnp.float32
            )
            * scaling
        )
        grad_keys = (
            jnp.einsum("sqhk,sqhd->skhd", grad_scores, queries, preferred_element_type=jnp.float32)
            * scaling
        )
        grad_values = jnp.einsum(
            "sqhk,sqhd->skhd",
            soft_probs.astype(jnp.bfloat16),
            grad_attended,
            preferred_element_type=jnp.float32,
        )
        key_term = jnp.concatenate(
            [
                grad_keys.reshape(seq_count, block_width, model_width),
                grad_values.reshape(seq_count, block_width, model_width),
            ],
            axis=-1,
        )
        return (grad_queries, key_term)

    grad_queries, key_terms = lax.scan(
        back_block, zero_queries, jnp.arange(block_count, dtype=jnp.int32)
    )
    own_terms = lax.psum_scatter(
        key_terms.astype(jnp.bfloat16), "ctx", scatter_dimension=0, tiled=True
    ).astype(jnp.float32)
    own_terms = own_terms.transpose(1, 0, 2, 3).reshape(row_count, 2 * model_width)
    grad_qkv = jnp.concatenate(
        [grad_queries.reshape(row_count, model_width), own_terms], axis=-1
    ).astype(jnp.bfloat16)
    grad_qkv_w = jnp.einsum("rd,re->de", hidden_one, grad_qkv, preferred_element_type=jnp.float32)
    column_sums = jnp.sum(grad_qkv.astype(jnp.float32), axis=0)
    grad_qv_bias = jnp.stack([column_sums[:model_width], column_sums[2 * model_width :]])
    grad_hidden_one = jnp.einsum(
        "re,de->rd", grad_qkv, whole_qkv, preferred_element_type=jnp.float32
    )
    grad_gain_one = jnp.sum(grad_hidden_one * normed_one, axis=0)
    grad_shift_one = jnp.sum(grad_hidden_one, axis=0)
    grad_inputs = (
        (
            grad_middle
            + norm_back(grad_hidden_one, normed_one, scale_one, gain_one.astype(jnp.float32))
        )
        .astype(jnp.bfloat16)
        .reshape(seq_count, local_len, model_width)
    )
    owned = (
        lax.psum_scatter(
            grad_qkv_w.astype(jnp.bfloat16), "fsdp", scatter_dimension=0, tiled=True
        ).astype(jnp.float32),
        lax.psum_scatter(
            grad_out.astype(jnp.bfloat16), "fsdp", scatter_dimension=0, tiled=True
        ).astype(jnp.float32),
        lax.psum_scatter(
            grad_up.astype(jnp.bfloat16), "fsdp", scatter_dimension=0, tiled=True
        ).astype(jnp.float32),
        lax.psum_scatter(
            grad_down.astype(jnp.bfloat16), "fsdp", scatter_dimension=0, tiled=True
        ).astype(jnp.float32),
        lax.psum_scatter(
            grad_qv_bias.astype(jnp.bfloat16), "fsdp", scatter_dimension=1, tiled=True
        ).astype(jnp.float32),
        lax.psum_scatter(
            grad_out_bias.astype(jnp.bfloat16), "fsdp", scatter_dimension=0, tiled=True
        ).astype(jnp.float32),
        lax.psum_scatter(
            grad_up_bias.astype(jnp.bfloat16), "fsdp", scatter_dimension=0, tiled=True
        ).astype(jnp.float32),
        lax.psum_scatter(
            grad_down_bias.astype(jnp.bfloat16), "fsdp", scatter_dimension=0, tiled=True
        ).astype(jnp.float32),
        lax.psum_scatter(
            grad_gain_one.astype(jnp.bfloat16), "fsdp", scatter_dimension=0, tiled=True
        ).astype(jnp.float32),
        lax.psum_scatter(
            grad_shift_one.astype(jnp.bfloat16), "fsdp", scatter_dimension=0, tiled=True
        ).astype(jnp.float32),
        lax.psum_scatter(
            grad_gain_two.astype(jnp.bfloat16), "fsdp", scatter_dimension=0, tiled=True
        ).astype(jnp.float32),
        lax.psum_scatter(
            grad_shift_two.astype(jnp.bfloat16), "fsdp", scatter_dimension=0, tiled=True
        ).astype(jnp.float32),
    )
    summed = lax.psum(
        (
            owned[0],
            owned[1],
            owned[2],
            owned[3],
            owned[4],
            owned[5],
            owned[6],
            owned[7],
            owned[8],
            owned[9],
            owned[10],
            owned[11],
        ),
        ("dp", "ctx"),
    )
    return (
        outputs,
        grad_inputs,
        summed[0],
        summed[1],
        summed[2],
        summed[3],
        summed[4],
        summed[5],
        summed[6],
        summed[7],
        summed[8],
        summed[9],
        summed[10],
        summed[11],
    )


def solution(mesh):
    return jax.shard_map(
        body,
        mesh=mesh,
        in_specs=(
            P(("dp", "fsdp"), "ctx", None),
            P(("dp", "fsdp"), "ctx", None),
            P(),
            P("fsdp", None),
            P("fsdp", None),
            P("fsdp", None),
            P("fsdp", None),
            P(None, "fsdp"),
            P("fsdp"),
            P("fsdp"),
            P("fsdp"),
            P("fsdp"),
            P("fsdp"),
            P("fsdp"),
            P("fsdp"),
        ),
        out_specs=(
            P(("dp", "fsdp"), "ctx", None),
            P(("dp", "fsdp"), "ctx", None),
            P("fsdp", None),
            P("fsdp", None),
            P("fsdp", None),
            P("fsdp", None),
            P(None, "fsdp"),
            P("fsdp"),
            P("fsdp"),
            P("fsdp"),
            P("fsdp"),
            P("fsdp"),
            P("fsdp"),
            P("fsdp"),
        ),
        check_vma=False,
    )
```

profile of v0, /device:TPU:9, one launch (start us, length us, event | category | flops | bytes accessed | tf_op | source)
XLA Modules:
  0.0 861.1 jit_solution(11961605352511192800)
XLA Ops:
  8.0 1.3 fusion.91
  14.2 12.6 %all-reduce.15 = (bf16[768]{0:T(1024)(128)(2,1)S(1)}, bf16[768]{0:T(1024)(128)(2,1)S(1)}, bf16[768]{0:T(1024)(128)(2,1)S(1)}, bf16[768]{0:T(1024)(128)(2,1)S(1)}, bf16[768]{0:T(1024)(128)(2,1)S(1)}) all-reduce(bf16[768]{0:T(1024)(128)(2,1)S(1)} %dynamic-update-slice.1, ...), channel_id=1, replica_groups=mesh['dp'=4,'fsdp'=4,'ctx'=2] {'fsdp'}, use_global_device_ids=true, to_apply=%add.1 | all-reduce | flops 3840 | bytes 15360
  26.7 9.8 %all-gather.2 = bf16[4,192,2]{1,2,0:T(2,128)(2,1)S(1)} all-gather(bf16[1,192,2]{1,2,0:T(2,128)(2,1)} %bitcast.311), channel_id=1, replica_groups=mesh['dp'=4,'fsdp'=4,'ctx'=2] {'fsdp'}, dimensions={0}, use_global_device_ids=true | all-gather | bytes 3840 | tf_op jit(solution)/shard_map/all_gather | solution.py:115
  36.7 1.3 convert_reduce_fusion
  38.4 40.3 %all-gather.11.cloned.1.call-done = bf16[768,2304]{1,0:T(8,128)(2,1)} async-done(((bf16[192,2304]{1,0:T(8,128)(2,1)}), bf16[768,2304]{1,0:T(8,128)(2,1)}) %all-gather.11.cloned.1.call-update) | async-done | bytes 3538960 | tf_op jit(solution)/shard_map/all_gather | solution.py:111
  78.8 4.1 fusion.87
  83.0 1.4 fusion.66
  85.4 2.4 slice.47
  89.8 10.5 %all-gather.3 = bf16[4,1,768]{2,1,0:T(2,128)(2,1)S(1)} all-gather(bf16[1,1,768]{2,1,0:T(2,128)(2,1)S(1)} %reshape.501), channel_id=1, replica_groups=mesh['dp'=4,'fsdp'=4,'ctx'=2] {'fsdp'}, dimensions={0}, use_global_device_ids=true | all-gather | bytes 7680 | tf_op jit(solution)/shard_map/all_gather | solution.py:117
  101.5 2.6 copy.81
  104.1 6.1 all-gather.19.cloned.1.call-done
  110.2 2.6 copy.80
  112.8 42.6 %while.35 = (s32[]{:T(128)}, f32[1,512,12]{1,2,0:T(8,128)S(1)}, f32[1,512,12]{1,2,0:T(8,128)S(1)}, f32[1,512,12,64]{1,3,2,0:T(8,128)S(1)}, s32[4]{0:T(128)S(1)},...) while((s32[]{:T(128)}, f32[1,512,12]{1,2,0:T(8,128)S(1)}, ...), condition=%wide.region_7.8_spmd.clone, body=%wide.region_3.7_spmd.clone.sunk | while | flops 847700480 | bytes 98187504 | solution.py:86
  112.8 1.5 constant_dynamic-slice_fusion.6
  114.6 7.8 fusion.139
  122.4 6.5 bitcast_add_fusion.7
  128.9 1.7 copy-done
  130.6 3.1 fusion.141
  133.8 1.5 constant_dynamic-slice_fusion.6
  135.7 7.8 fusion.139
  143.5 6.5 bitcast_add_fusion.7
  150.0 2.2 copy-done
  152.2 3.1 fusion.141
  155.6 2.5 fusion.92
  159.6 70.3 %all-gather.15.cloned.1.call-done = bf16[768,3072]{1,0:T(8,128)(2,1)} async-done(((bf16[192,3072]{1,0:T(8,128)(2,1)}), bf16[768,3072]{1,0:T(8,128)(2,1)}) %all-gather.15.cloned.1.call-update) | async-done | bytes 4718608 | tf_op jit(solution)/shard_map/all_gather | solution.py:113
  229.9 8.2 fusion.89
  238.1 81.1 %all-gather.17.cloned.1.call-done = bf16[3072,768]{1,0:T(8,128)(2,1)} async-done(((bf16[768,768]{1,0:T(8,128)(2,1)}), bf16[3072,768]{1,0:T(8,128)(2,1)}) %all-gather.17.cloned.1.call-update) | async-done | bytes 4718608 | tf_op jit(solution)/shard_map/all_gather | solution.py:114
  319.2 11.3 %fusion.93 = (bf16[3072]{0:T(1024)(128)(2,1)}, bf16[512,3072]{1,0:T(8,128)(2,1)S(1)}) fusion(bf16[3072,768]{1,0:T(8,128)(2,1)} %all-gather.17.cloned.1.call-done, bf16[1,512,768]{2,1,0:T(8,128)(2,1)S(1)} %copy-done.18, f32[512,3072]{1,0:T(8,128)} %fusion.89, f32[3072]{0:T(1024)S(1)} %bitcast.308), kind=kOutput, calls=%fused_computation.179 | convolution fusion | flops 2456810496 | bytes 14960640 | tf_op jit(solution)/shard_map/rd,fd->rf/dot_general | solution.py:214
  330.5 3.5 multiply_reduce_fusion
  334.1 1.3 convert_reduce_fusion.1
  335.3 1.2 copy-done.7
  338.5 1.4 multiply_reduce_fusion.1
  340.0 61.1 %while.36 = (s32[]{:T(128)}, f32[1,512,12,64]{1,3,2,0:T(8,128)}, bf16[2,1,512,1536]{2,3,1,0:T(8,128)(2,1)}, s32[2]{0:T(128)S(1)}, bf16[1,1024,768]{1,2,0:T(8,128...) while((s32[]{:T(128)}, f32[1,512,12,64]{1,3,2,0:T(8,128)}, ...), condition=%wide.region_15.16_spmd.clone, body=%wide.region_13.15_spmd.clone.sunk | while | flops 2056409600 | bytes 118053760 | solution.py:323
  341.7 2.4 constant_dynamic-slice_fusion.7
  344.1 3.2 fusion.152
  347.7 5.5 fusion.154
  353.2 4.6 convolution_multiply_fusion.2
  357.8 5.0 fusion.155
  362.9 2.9 fusion.156
  365.7 3.9 bitcast_add_fusion.8
  372.1 2.4 constant_dynamic-slice_fusion.7
  374.5 3.2 fusion.152
  378.1 5.5 fusion.154
  383.6 4.6 convolution_multiply_fusion.2
  388.2 5.0 fusion.155
  393.2 2.8 fusion.156
  396.0 3.9 bitcast_add_fusion.8
  401.2 1.3 copy-done.8
  402.5 2.9 convolution_convert_fusion.3
  406.5 7.5 reduce-scatter.9.cloned.1.call-done
  414.0 2.0 fusion.75
  417.0 6.7 convolution_convert_fusion.1
  424.8 8.7 %convolution_convert_fusion = bf16[3072,768]{1,0:T(8,128)(2,1)} fusion(bf16[1,512,768]{2,1,0:T(8,128)(2,1)S(1)} %copy-done.19, f32[512,3072]{1,0:T(8,128)} %fusion.89, f32[3072]{0:T(1024)S(1)} %bitcast.309), kind=kOutput, calls=%fused_computation.86 | convolution fusion | flops 2434007040 | bytes 11808768 | tf_op jit(solution)/shard_map/rf,rd->fd/dot_general | solution.py:212
  434.9 5.5 convolution_convert_fusion.2
  440.4 1.3 reduce_sum.228
  443.3 1.3 reduce-scatter.13.cloned.1.call-done
  444.6 6.0 fusion.63
  450.6 13.8 %all-reduce.14 = (bf16[768]{0:T(1024)(128)(2,1)S(1)}, bf16[768]{0:T(1024)(128)(2,1)S(1)}, bf16[3072]{0:T(1024)(128)(2,1)S(1)}, bf16[768]{0:T(1024)(128)(2,1)S(1)...) all-reduce(bf16[768]{0:T(1024)(128)(2,1)S(1)} %dynamic-update-slice, ...), channel_id=1, replica_groups=mesh['dp'=4,'fsdp'=4,'ctx'=2] {'fsdp'}, use_global_device_ids=true, to_apply=%add.5 | all-reduce | flops 8448 | bytes 33792
  464.9 3.0 fusion.69
  467.9 9.0 %fusion.68 = bf16[1,512,768]{2,1,0:T(8,128)(2,1)} fusion(f32[512,768]{1,0:T(8,128)S(1)} %copy-done.14, bf16[3072,768]{1,0:T(8,128)(2,1)} %all-gather.17.cloned.1.call-done, f32[768]{0:T(1024)S(1)} %convert_element_type.200, f32[512,3072]{1,0:T(8,128)} %fusion.89, f32[3072]{0:T(1024)S(1)} %bitcast.310), kind=kOutput, calls=%fused_computation.127 | convolution fusion | flops 2432827392 | bytes 13384704 | tf_op jit(solution)/shard_map/dot_general | solution.py:198
  477.8 75.6 %reduce-scatter.15.cloned.1.call-done = bf16[192,3072]{1,0:T(8,128)(2,1)} async-done(((bf16[768,3072]{1,0:T(8,128)(2,1)}), bf16[192,3072]{1,0:T(8,128)(2,1)}) %reduce-scatter.15.cloned.1.call-update) | async-done | bytes 1179664 | tf_op jit(solution)/shard_map/reduce_scatter | solution.py:356
  553.4 88.1 %reduce-scatter.17.cloned.1.call-done = bf16[768,768]{1,0:T(8,128)(2,1)} async-done(((bf16[3072,768]{1,0:T(8,128)(2,1)}), bf16[768,768]{1,0:T(8,128)(2,1)}) %reduce-scatter.17.cloned.1.call-update) | async-done | bytes 1179664 | tf_op jit(solution)/shard_map/reduce_scatter | solution.py:359
  641.5 68.9 %reduce-scatter.11.cloned.1.call-done = bf16[192,2304]{1,0:T(8,128)(2,1)} async-done(((bf16[768,2304]{1,0:T(8,128)(2,1)}), bf16[192,2304]{1,0:T(8,128)(2,1)}) %reduce-scatter.11.cloned.1.call-update) | async-done | bytes 884752 | tf_op jit(solution)/shard_map/reduce_scatter | solution.py:350
  710.4 143.6 %all-reduce.17 = (f32[192,2304]{1,0:T(8,128)}, f32[192,768]{1,0:T(8,128)}, f32[192,3072]{1,0:T(8,128)}, f32[768,768]{1,0:T(8,128)}, f32[2,192]{1,0:T(2,128)}, /*...) all-reduce(bf16[192,2304]{1,0:T(8,128)(2,1)} %reduce-scatter.11.clo, ...), channel_id=1, replica_groups=mesh['dp'=4,'fsdp'=4,'ctx'=2] {'dp','ctx'}, use_global_device_ids=true, to_apply=%region_20.21 | all-reduce | flops 1771776 | bytes 10634496 | tf_op jit(solution)/shard_map/psum | solution.py:387
  (201 shorter events, 24.4 us)
Async XLA Ops:
  7.2 30.8 %copy-start.9 = (bf16[1,512,768]{2,1,0:T(8,128)(2,1)S(1)}, bf16[1,512,768]{2,1,0:T(8,128)(2,1)}, u32[]{:S(2)}) copy-start(bf16[1,512,768]{2,1,0:T(8,128)(2,1)} %param.19) | copy-start | bytes 2359300
  7.2 71.6 %all-gather.11.cloned.1.call-start = ((), (), s32[]{:S(2)}) async-start(), calls=%async_computation.6 | async-start | bytes 4423680 | tf_op jit(solution)/shard_map/all_gather | solution.py:111
  7.9 93.6 %all-gather.21.cloned.1.call-start = ((), (), s32[]{:S(2)}) async-start(), calls=%async_computation.16 | async-start | bytes 2359296 | tf_op jit(solution)/shard_map/all_gather | solution.py:171
  26.7 56.2 %copy-start.24 = (f32[768]{0:T(1024)}, f32[768]{0:T(1024)S(1)}, u32[]{:S(2)}) copy-start(f32[768]{0:T(1024)S(1)} %convert_element_type.186) | copy-start | bytes 9220
  26.7 56.2 %copy-start.30 = (f32[768]{0:T(1024)}, f32[768]{0:T(1024)S(1)}, u32[]{:S(2)}) copy-start(f32[768]{0:T(1024)S(1)} %convert_element_type.187) | copy-start | bytes 9220
  38.0 44.9 %copy-start.22 = (f32[512]{0:T(512)}, f32[512]{0:T(512)S(1)}, u32[]{:S(2)}) copy-start(f32[512]{0:T(512)S(1)} %broadcast_multiply_fusion.5) | copy-start | bytes 6148
  38.4 44.5 %copy-start.27 = (f32[512]{0:T(512)}, f32[512]{0:T(512)S(1)}, u32[]{:S(2)}) copy-start(f32[512]{0:T(512)S(1)} %add_rsqrt_fusion.1) | copy-start | bytes 6148
  82.9 2.4 copy-start.15
  85.3 4.3 copy-start.21
  85.3 4.4 copy-start.36
  85.4 24.8 %all-gather.19.cloned.1.call-start = ((), (), s32[]{:S(2)}) async-start(), calls=%async_computation.15 | async-start | bytes 2359296 | tf_op jit(solution)/shard_map/all_gather | solution.py:170
  87.8 67.8 %all-gather.13.cloned.1.call-start = ((), (), s32[]{:S(2)}) async-start(), calls=%async_computation.7 | async-start | bytes 1474560 | tf_op jit(solution)/shard_map/all_gather | solution.py:112
  88.4 141.5 %all-gather.15.cloned.1.call-start = ((), (), s32[]{:S(2)}) async-start(), calls=%async_computation.8 | async-start | bytes 5898240 | tf_op jit(solution)/shard_map/all_gather | solution.py:113
  89.0 230.3 %all-gather.17.cloned.1.call-start = ((), (), s32[]{:S(2)}) async-start(), calls=%async_computation.9 | async-start | bytes 5898240 | tf_op jit(solution)/shard_map/all_gather | solution.py:114
  89.5 324.4 %reduce-scatter.9.cloned.1.call-start = ((), (), s32[]{:S(2)}) async-start(), calls=%async_computation.10 | async-start | bytes 4718592 | tf_op jit(solution)/shard_map/reduce_scatter | solution.py:326
  89.8 140.1 %copy-start.32 = (f32[768]{0:T(1024)}, f32[768]{0:T(1024)S(1)}, u32[]{:S(2)}) copy-start(f32[768]{0:T(1024)S(1)} %convert_element_type.196) | copy-start | bytes 9220
  122.3 8.3 copy-start
  143.5 8.7 %copy-start = (f32[12,512,512]{2,1,0:T(8,128)S(1)}, f32[12,512,512]{2,1,0:T(8,128)}, u32[]{:S(2)}) copy-start(f32[12,512,512]{2,1,0:T(8,128)} %get-tuple-element.799) | copy-start | bytes 37748740 | tf_op jit(solution)/shard_map/while
  155.6 2.5 copy-start.16
  158.1 1.1 copy-start.11
  159.6 159.6 %copy-start.18 = (bf16[1,512,768]{2,1,0:T(8,128)(2,1)S(1)}, bf16[1,512,768]{2,1,0:T(8,128)(2,1)}, u32[]{:S(2)}) copy-start(bf16[1,512,768]{2,1,0:T(8,128)(2,1)} %param.20) | copy-start | bytes 2359300
  319.2 11.3 %copy-start.12 = (f32[512,768]{1,0:T(8,128)S(1)}, f32[512,768]{1,0:T(8,128)}, u32[]{:S(2)}) copy-start(f32[512,768]{1,0:T(8,128)} %copy-done.11) | copy-start | bytes 4718596
  319.2 11.3 %copy-start.37 = (bf16[768,3072]{1,0:T(8,128)(2,1)S(1)}, bf16[768,3072]{1,0:T(8,128)(2,1)}, u32[]{:S(2)}) copy-start(bf16[768,3072]{1,0:T(8,128)(2,1)} %all-gather.15.cloned.1.call-done) | copy-start | bytes 14155780
  330.5 3.6 copy-start.40
  334.1 2.5 copy-start.38
  335.3 1.2 copy-start.7
  344.1 3.3 copy-start.1
  353.2 4.6 copy-start.3
  362.8 2.9 copy-start.2
  362.8 2.9 copy-start.4
  369.7 1.1 copy-start.5
  374.5 3.3 copy-start.1
  383.6 4.6 copy-start.3
  393.2 2.8 copy-start.2
  393.2 2.8 copy-start.4
  399.9 1.1 copy-start.5
  401.1 1.4 copy-start.8
  401.1 4.4 copy-start.6
  401.1 43.5 %reduce-scatter.13.cloned.1.call-start = ((), (), s32[]{:S(2)}) async-start(), calls=%async_computation.12 | async-start | bytes 1474560 | tf_op jit(solution)/shard_map/reduce_scatter | solution.py:353
  405.4 71.5 %reduce-scatter.19.cloned.1.call-start = ((), (), s32[]{:S(2)}) async-start(), calls=%async_computation.17 | async-start | bytes 245760
  405.5 11.4 %copy-start.33 = (f32[768]{0:T(1024)S(1)}, f32[768]{0:T(1024)}, u32[]{:S(2)}) copy-start(f32[768]{0:T(1024)} %copy-done.32) | copy-start | bytes 9220
  406.5 10.4 %copy-start.13 = (f32[512,768]{1,0:T(8,128)S(1)}, f32[512,768]{1,0:T(8,128)}, u32[]{:S(2)}) copy-start(f32[512,768]{1,0:T(8,128)} %copy-done.11) | copy-start | bytes 4718596
  416.9 136.5 %reduce-scatter.15.cloned.1.call-start = ((), (), s32[]{:S(2)}) async-start(), calls=%async_computation.13 | async-start | bytes 5898240 | tf_op jit(solution)/shard_map/reduce_scatter | solution.py:356
  423.6 1.2 copy-start.19
  423.7 217.8 %reduce-scatter.17.cloned.1.call-start = ((), (), s32[]{:S(2)}) async-start(), calls=%async_computation.14 | async-start | bytes 5898240 | tf_op jit(solution)/shard_map/reduce_scatter | solution.py:359
  433.5 1.1 copy-start.10
  433.5 1.4 copy-start.17
  433.5 1.4 copy-start.23
  433.5 1.4 copy-start.25
  433.5 1.4 copy-start.28
  433.5 1.4 copy-start.31
  433.6 276.8 %reduce-scatter.11.cloned.1.call-start = ((), (), s32[]{:S(2)}) async-start(), calls=%async_computation.11 | async-start | bytes 4423680 | tf_op jit(solution)/shard_map/reduce_scatter | solution.py:350
  440.4 2.6 copy-start.39
  443.3 7.3 copy-start.26
  443.3 7.3 copy-start.29
  443.3 7.3 copy-start.34
  443.3 7.3 copy-start.35
  464.9 3.0 copy-start.14
  467.9 242.5 %copy-start.20 = (bf16[192,768]{1,0:T(8,128)(2,1)S(1)}, bf16[192,768]{1,0:T(8,128)(2,1)}, u32[]{:S(2)}) copy-start(bf16[192,768]{1,0:T(8,128)(2,1)} %reduce-scatter.13.cloned.1.call-done) | copy-start | bytes 884740
Sparse Core Ops, SparseCore 0:
  9.6 69.1 all-gather.10
  85.5 11.5 all-gather.20
  99.2 10.9 all-gather.18
  111.6 30.1 all-gather.12
  143.2 86.6 all-gather.14
  231.3 87.8 all-gather.16
  401.2 12.6 reduce-scatter.8
  417.0 27.5 reduce-scatter.12
  447.5 15.4 reduce-scatter.18
  465.2 88.1 reduce-scatter.14
  555.7 85.7 reduce-scatter.16
  643.7 66.6 reduce-scatter.10
where the time goes:
time: 869 us; the launch traced here: 861 us
  waiting for transfers between devices  442 us (51%)
  blocking collectives  190 us (22%)
  matrix products  142 us (16%)
  local copies, waits for them, and re-layouts  39.7 us (5%)
  other arithmetic  27.6 us (3%)
  between operations  16.9 us (2%)
    psum x1, blocking collectives, body(): lax.psum((owned[0], owned[1], owned[2], owned[3], owned[4], owned[5], own...  144 us
    reduce_scatter x1, waiting for transfers between devices, body(): lax.psum_scatter(grad_down.astype(jnp.bfloat16), 'fsdp', scatter_dimensio...  88.1 us
    all_gather x1, waiting for transfers between devices, body(): lax.all_gather(w_down, 'fsdp', axis=0, tiled=True)  81.1 us
    reduce_scatter x1, waiting for transfers between devices, body(): lax.psum_scatter(grad_up.astype(jnp.bfloat16), 'fsdp', scatter_dimension=...  75.6 us
    all_gather x1, waiting for transfers between devices, body(): lax.all_gather(w_up, 'fsdp', axis=0, tiled=True)  70.3 us
    reduce_scatter x1, waiting for transfers between devices, body(): lax.psum_scatter(grad_qkv_w.astype(jnp.bfloat16), 'fsdp', scatter_dimensi...  68.9 us
    all_gather x1, waiting for transfers between devices, body(): lax.all_gather(w_qkv, 'fsdp', axis=0, tiled=True)  40.3 us
    unnamed x2, blocking collectives  26.3 us
  transfers between devices with their start and end apart: 12, of which 9 were waited for; matrix products, arithmetic and copies ran while one was open for 13% of the time, Pallas kernels for 0%

commit v1 on v0

--- a/solution.py
+++ b/solution.py
@@ -107,34 +107,50 @@
     row_count = seq_count * local_len
     piece_len = local_len // 2
     scaling = HD ** (-0.5)
-    gathered_weights = (
-        lax.all_gather(w_qkv, "fsdp", axis=0, tiled=True),
-        lax.all_gather(w_out, "fsdp", axis=0, tiled=True),
-        lax.all_gather(w_up, "fsdp", axis=0, tiled=True),
-        lax.all_gather(w_down, "fsdp", axis=0, tiled=True),
-        lax.all_gather(qv_bias, "fsdp", axis=1, tiled=True),
-        lax.all_gather(out_bias, "fsdp", axis=0, tiled=True),
-        lax.all_gather(up_bias, "fsdp", axis=0, tiled=True),
-        lax.all_gather(down_bias, "fsdp", axis=0, tiled=True),
-        lax.all_gather(norm1_gain, "fsdp", axis=0, tiled=True),
-        lax.all_gather(norm1_shift, "fsdp", axis=0, tiled=True),
-        lax.all_gather(norm2_gain, "fsdp", axis=0, tiled=True),
-        lax.all_gather(norm2_shift, "fsdp", axis=0, tiled=True),
-    )
-    (
-        whole_qkv,
-        whole_out,
-        whole_up,
-        whole_down,
-        whole_qv,
-        whole_ob,
-        whole_ub,
-        whole_db,
-        gain_one,
-        shift_one,
-        gain_two,
-        shift_two,
-    ) = gathered_weights
+    spread = ("fsdp", "dp", "ctx")
+    copies = lax.axis_size("dp") * lax.axis_size("ctx")
+    copy_index = lax.axis_index("dp") * lax.axis_size("ctx") + lax.axis_index("ctx")
+
+    def own_piece(shard):
+        rows = shard.shape[0] // copies
+        return lax.dynamic_slice_in_dim(shard, copy_index * rows, rows, 0)
+
+    def gather_whole(shard):
+        return lax.all_gather(own_piece(shard), spread, axis=0, tiled=True)
+
+    shards = lax.axis_size("fsdp")
+    small_row = jnp.concatenate(
+        [
+            qv_bias.reshape(-1),
+            out_bias,
+            up_bias,
+            down_bias,
+            norm1_gain,
+            norm1_shift,
+            norm2_gain,
+            norm2_shift,
+        ]
+    )
+    small_rows = lax.all_gather(small_row, "fsdp", axis=0, tiled=False)
+    part = model_width // shards
+
+    def small_part(start, width):
+        return small_rows[:, start : start + width].reshape(-1)
+
+    whole_qv = jnp.stack([small_part(0, part), small_part(part, part)])
+    whole_ob = small_part(2 * part, part)
+    hidden_part = up_bias.shape[0]
+    whole_ub = small_part(3 * part, hidden_part)
+    rest = 3 * part + hidden_part
+    whole_db = small_part(rest, part)
+    gain_one = small_part(rest + part, part)
+    shift_one = small_part(rest + 2 * part, part)
+    gain_two = small_part(rest + 3 * part, part)
+    shift_two = small_part(rest + 4 * part, part)
+    whole_qkv = gather_whole(w_qkv)
+    whole_out = gather_whole(w_out)
+    whole_up = gather_whole(w_up)
+    whole_down = gather_whole(w_down)
     flat_in = inputs.reshape(row_count, model_width).astype(jnp.float32)
     normed_one, scale_one = normalize(flat_in)
     hidden_one = (normed_one * gain_one.astype(jnp.float32) + shift_one.astype(jnp.float32)).astype(
@@ -199,14 +215,6 @@
         + whole_db.astype(jnp.float32)
     )
     outputs = result.astype(jnp.bfloat16).reshape(seq_count, local_len, model_width)
-    whole_qkv, whole_out, whole_up, whole_down, gain_one, gain_two = (
-        lax.all_gather(w_qkv, "fsdp", axis=0, tiled=True),
-        lax.all_gather(w_out, "fsdp", axis=0, tiled=True),
-        lax.all_gather(w_up, "fsdp", axis=0, tiled=True),
-        lax.all_gather(w_down, "fsdp", axis=0, tiled=True),
-        lax.all_gather(norm1_gain, "fsdp", axis=0, tiled=True),
-        lax.all_gather(norm2_gain, "fsdp", axis=0, tiled=True),
-    )
     grad_rows = cotangent.reshape(row_count, model_width)
     grad_rows_f32 = grad_rows.astype(jnp.float32)
     grad_down = jnp.einsum("rf,rd->fd", activated, grad_rows, preferred_element_type=jnp.float32)
@@ -346,76 +354,64 @@
         .astype(jnp.bfloat16)
         .reshape(seq_count, local_len, model_width)
     )
-    owned = (
-        lax.psum_scatter(
-            grad_qkv_w.astype(jnp.bfloat16), "fsdp", scatter_dimension=0, tiled=True
-        ).astype(jnp.float32),
-        lax.psum_scatter(
-            grad_out.astype(jnp.bfloat16), "fsdp", scatter_dimension=0, tiled=True
-        ).astype(jnp.float32),
-        lax.psum_scatter(
-            grad_up.astype(jnp.bfloat16), "fsdp", scatter_dimension=0, tiled=True
-        ).astype(jnp.float32),
-        lax.psum_scatter(
-            grad_down.astype(jnp.bfloat16), "fsdp", scatter_dimension=0, tiled=True
-        ).astype(jnp.float32),
-        lax.psum_scatter(
-            grad_qv_bias.astype(jnp.bfloat16), "fsdp", scatter_dimension=1, tiled=True
-        ).astype(jnp.float32),
-        lax.psum_scatter(
-            grad_out_bias.astype(jnp.bfloat16), "fsdp", scatter_dimension=0, tiled=True
-        ).astype(jnp.float32),
-        lax.psum_scatter(
-            grad_up_bias.astype(jnp.bfloat16), "fsdp", scatter_dimension=0, tiled=True
-        ).astype(jnp.float32),
-        lax.psum_scatter(
-            grad_down_bias.astype(jnp.bfloat16), "fsdp", scatter_dimension=0, tiled=True
-        ).astype(jnp.float32),
-        lax.psum_scatter(
-            grad_gain_one.astype(jnp.bfloat16), "fsdp", scatter_dimension=0, tiled=True
-        ).astype(jnp.float32),
-        lax.psum_scatter(
-            grad_shift_one.astype(jnp.bfloat16), "fsdp", scatter_dimension=0, tiled=True
-        ).astype(jnp.float32),
-        lax.psum_scatter(
-            grad_gain_two.astype(jnp.bfloat16), "fsdp", scatter_dimension=0, tiled=True
-        ).astype(jnp.float32),
-        lax.psum_scatter(
-            grad_shift_two.astype(jnp.bfloat16), "fsdp", scatter_dimension=0, tiled=True
-        ).astype(jnp.float32),
-    )
-    summed = lax.psum(
-        (
-            owned[0],
-            owned[1],
-            owned[2],
-            owned[3],
-            owned[4],
-            owned[5],
-            owned[6],
-            owned[7],
-            owned[8],
-            owned[9],
-            owned[10],
-            owned[11],
-        ),
-        ("dp", "ctx"),
-    )
+    def share(grad):
+        piece = lax.psum_scatter(
+            grad.astype(jnp.bfloat16), spread, scatter_dimension=0, tiled=True
+        )
+        return lax.all_gather(piece, ("dp", "ctx"), axis=0, tiled=True).astype(jnp.float32)
+
+    small_grads = jnp.concatenate(
+        [
+            grad_qv_bias[0].reshape(shards, part),
+            grad_qv_bias[1].reshape(shards, part),
+            grad_out_bias.reshape(shards, part),
+            grad_up_bias.reshape(shards, hidden_part),
+            grad_down_bias.reshape(shards, part),
+            grad_gain_one.reshape(shards, part),
+            grad_shift_one.reshape(shards, part),
+            grad_gain_two.reshape(shards, part),
+            grad_shift_two.reshape(shards, part),
+        ],
+        axis=1,
+    )
+    small_width = small_grads.shape[1]
+    piece_width = small_width // copies
+    out_rows = model_width // (shards * copies)
+    packed = jnp.concatenate(
+        [
+            grad_out.astype(jnp.bfloat16).reshape(shards * copies, out_rows, model_width),
+            jnp.pad(
+                small_grads.astype(jnp.bfloat16).reshape(shards * copies, 1, piece_width),
+                ((0, 0), (0, 7), (0, model_width - piece_width)),
+            ),
+        ],
+        axis=1,
+    )
+    own_down = share(grad_down)
+    own_up = share(grad_up)
+    own_qkv = share(grad_qkv_w)
+    own_packed = share(packed)
+    own_out = own_packed[:, :out_rows].reshape(copies * out_rows, model_width)
+    own_small = own_packed[:, out_rows, :piece_width].reshape(small_width)
+
+    def own_part(start, width):
+        return own_small[start : start + width]
+
     return (
         outputs,
         grad_inputs,
-        summed[0],
-        summed[1],
-        summed[2],
-        summed[3],
-        summed[4],
-        summed[5],
-        summed[6],
-        summed[7],
-        summed[8],
-        summed[9],
-        summed[10],
-        summed[11],
+        own_qkv,
+        own_out,
+        own_up,
+        own_down,
+        own_part(0, 2 * part).reshape(2, part),
+        own_part(2 * part, part),
+        own_part(3 * part, hidden_part),
+        own_part(rest, part),
+        own_part(rest + part, part),
+        own_part(rest + 2 * part, part),
+        own_part(rest + 3 * part, part),
+        own_part(rest + 4 * part, part),
     )
 
 

time: 869 us -> 829 us (0.954)
  blocking collectives: 190 us -> 35.8 us
  waiting for transfers between devices: 442 us -> 559 us
  matrix products: 142 us -> 128 us
  local copies, waits for them, and re-layouts: 39.7 us -> 48.7 us
    psum x1 -> x0, blocking collectives: 144 us -> none  [body(): lax.psum((owned[0], owned[1], owned[2], owned[3], owned[4], owned[5], own...]
    reduce_scatter x4, waiting for transfers between devices: 234 us -> 322 us  [share(): lax.psum_scatter(grad.astype(jnp.bfloat16), spread, scatter_dimension=0,...]
    unnamed x2 -> x0, blocking collectives: 26.3 us -> none
    all_gather x4 -> x6, waiting for transfers between devices: 192 us -> 214 us  [the longest x4 193 us: gather_whole(): return lax.all_gather(own_piece(shard), spread, axis=0, tiled=True)]
    all_gather x2 -> x3, blocking collectives: 20.3 us -> 35.8 us  [the longest x2 25 us: share(): lax.all_gather(piece, ('dp', 'ctx'), axis=0, tiled=True).astype(jnp.float32)]
    dot_general x2, matrix products: 15.5 us -> 4.14 us  [one_block(): jnp.einsum('sqhd,skhd->sqhk', queries, key_block, preferred_element_type=...]
    unnamed x88 -> x62, local copies, waits for them, and re-layouts: 19.7 us -> 10.3 us
  transfers between devices with their start and end apart: 12 -> 13, of which waited for: 9 -> 12; matrix products, arithmetic and copies ran while one was open for 13% -> 21% of each run, Pallas kernels for 0% -> 0%
where the time goes in v1:
time: 829 us; the launch traced here: 824 us
  waiting for transfers between devices  559 us (67%)
  matrix products  128 us (15%)
  local copies, waits for them, and re-layouts  48.7 us (6%)
  blocking collectives  35.8 us (4%)
  other arithmetic  33.8 us (4%)
  between operations  14.5 us (2%)
    reduce_scatter x4, waiting for transfers between devices, share(): lax.psum_scatter(grad.astype(jnp.bfloat16), spread, scatter_dimension=0,...  322 us
    all_gather x4, waiting for transfers between devices, gather_whole(): return lax.all_gather(own_piece(shard), spread, axis=0, tiled=True)  193 us
    all_gather x2, blocking collectives, share(): lax.all_gather(piece, ('dp', 'ctx'), axis=0, tiled=True).astype(jnp.float32)  25 us
    all_gather x2, waiting for transfers between devices, share(): lax.all_gather(piece, ('dp', 'ctx'), axis=0, tiled=True).astype(jnp.float32)  21.3 us
    dot_general x2, matrix products, score_grads(): jnp.einsum('sqhd,skhd->sqhk', grad_block, value_block, preferred_element_...  16.8 us
  transfers between devices with their start and end apart: 13, of which 12 were waited for; matrix products, arithmetic and copies ran while one was open for 21% of the time, Pallas kernels for 0%

profile of v1, /device:TPU:9, one launch (start us, length us, event | category | flops | bytes accessed | tf_op | source)
XLA Modules:
  0.0 823.6 jit_solution(12766181250975240339)
XLA Ops:
  7.3 1.6 constant_dynamic-slice_fusion.7
  9.7 4.8 concatenate.20
  14.5 10.8 %all-gather.3 = bf16[4,1,2304]{2,1,0:T(2,128)(2,1)S(1)} all-gather(bf16[1,1,2304]{2,1,0:T(2,128)(2,1)S(1)} %reshape.616), channel_id=2, replica_groups=mesh['dp'=4,'fsdp'=4,'ctx'=2] {'fsdp'}, dimensions={0}, use_global_device_ids=true | all-gather | bytes 23040 | tf_op jit(solution)/shard_map/all_gather | solution.py:134
  27.7 1.5 fusion.68
  29.3 43.4 %all-gather.13.cloned.1.call-done = bf16[768,2304]{1,0:T(8,128)(2,1)} async-done(((bf16[24,2304]{1,0:T(8,128)(2,1)}), bf16[768,2304]{1,0:T(8,128)(2,1)}) %all-gather.13.cloned.1.call-update) | async-done | bytes 3538960 | tf_op jit(solution)/shard_map/all_gather | solution.py:119
  72.6 4.4 fusion.89
  79.5 2.4 slice.170
  84.2 1.6 constant_dynamic-slice_fusion.4
  87.1 2.0 all-gather.27.cloned.1.call-done
  89.1 1.7 copy.69
  90.8 11.4 %all-gather.25.cloned.1.call-done = bf16[1024,768]{1,0:T(8,128)(2,1)} async-done(((bf16[512,768]{1,0:T(8,128)(2,1)}), bf16[1024,768]{1,0:T(8,128)(2,1)}) %all-gather.25.cloned.1.call-update) | async-done | bytes 1572880 | tf_op jit(solution)/shard_map/all_gather | solution.py:186
  102.2 2.6 copy.68
  104.8 23.3 %while.35 = (s32[]{:T(128)}, f32[1,512,12]{1,2,0:T(8,128)S(1)}, f32[1,512,12]{1,2,0:T(8,128)S(1)}, f32[1,512,12,64]{1,3,2,0:T(8,128)}, s32[4]{0:T(128)S(1)}, /*i...) while((s32[]{:T(128)}, f32[1,512,12]{1,2,0:T(8,128)S(1)}, ...), condition=%wide.region_7.8_spmd.clone, body=%wide.region_3.7_spmd.clone.sunk | while | flops 847700480 | bytes 60438800 | solution.py:86
  106.4 2.1 fusion.141
  108.5 3.1 fusion.143
  111.7 3.6 bitcast_add_fusion.7
  118.0 2.1 fusion.141
  120.2 3.1 fusion.143
  123.3 3.6 bitcast_add_fusion.7
  128.1 2.6 fusion.79
  130.6 29.0 %all-gather.15.cloned.1.call-done = bf16[768,768]{1,0:T(8,128)(2,1)} async-done(((bf16[24,768]{1,0:T(8,128)(2,1)}), bf16[768,768]{1,0:T(8,128)(2,1)}) %all-gather.15.cloned.1.call-update) | async-done | bytes 1179664 | tf_op jit(solution)/shard_map/all_gather | solution.py:119
  159.6 2.4 fusion.94
  163.5 62.8 %all-gather.17.cloned.1.call-done = bf16[768,3072]{1,0:T(8,128)(2,1)} async-done(((bf16[24,3072]{1,0:T(8,128)(2,1)}), bf16[768,3072]{1,0:T(8,128)(2,1)}) %all-gather.17.cloned.1.call-update) | async-done | bytes 4718608 | tf_op jit(solution)/shard_map/all_gather | solution.py:119
  226.3 8.2 fusion.91
  234.4 57.6 %all-gather.19.cloned.1.call-done = bf16[3072,768]{1,0:T(8,128)(2,1)} async-done(((bf16[96,768]{1,0:T(8,128)(2,1)}), bf16[3072,768]{1,0:T(8,128)(2,1)}) %all-gather.19.cloned.1.call-update) | async-done | bytes 4718608 | tf_op jit(solution)/shard_map/all_gather | solution.py:119
  292.1 11.1 %fusion.95 = (bf16[3072]{0:T(1024)(128)(2,1)}, bf16[512,3072]{1,0:T(8,128)(2,1)S(1)}) fusion(bf16[3072,768]{1,0:T(8,128)(2,1)} %all-gather.19.cloned.1.call-done, bf16[1,512,768]{2,1,0:T(8,128)(2,1)S(1)} %copy-done.29, f32[512,3072]{1,0:T(8,128)} %fusion.91, f32[3072]{0:T(1024)S(1)} %reshape.611), kind=kOutput, calls=%fused_computation.191 | convolution fusion | flops 2456810496 | bytes 14960640 | tf_op jit(solution)/shard_map/rd,fd->rf/dot_general | solution.py:222
  303.2 1.6 copy-done.44
  304.9 4.9 convolution_convert_fusion.1
  309.9 6.8 multiply_reduce_fusion
  318.6 1.7 convolution_convert_fusion.4
  321.8 1.8 multiply_reduce_fusion.1
  323.6 8.9 %convolution_convert_fusion = bf16[3072,768]{1,0:T(8,128)(2,1)} fusion(bf16[1,512,768]{2,1,0:T(8,128)(2,1)S(1)} %copy-done.30, f32[512,3072]{1,0:T(8,128)} %fusion.91, f32[3072]{0:T(1024)S(1)} %reshape.611), kind=kOutput, calls=%fused_computation.91 | convolution fusion | flops 2434007040 | bytes 11808768 | tf_op jit(solution)/shard_map/rf,rd->fd/dot_general | solution.py:220
  332.8 62.0 %while.36 = (s32[]{:T(128)}, f32[1,512,12,64]{1,3,2,0:T(8,128)}, bf16[2,1,512,1536]{2,3,1,0:T(8,128)(2,1)}, s32[2]{0:T(128)S(1)}, bf16[1,1024,768]{1,2,0:T(8,128...) while((s32[]{:T(128)}, f32[1,512,12,64]{1,3,2,0:T(8,128)}, ...), condition=%wide.region_15.16_spmd.clone, body=%wide.region_13.15_spmd.clone.sunk | while | flops 2056409600 | bytes 171530928 | solution.py:331
  334.5 2.2 constant_dynamic-slice_fusion.11
  337.6 3.0 fusion.154
  340.6 5.1 fusion.157
  345.7 8.4 %fusion.156 = bf16[512,12,512]{0,2,1:T(8,128)(2,1)} fusion(f32[12,512,512]{2,1,0:T(8,128)S(1)} %fusion.154, f32[512,12]{0,1:T(8,128)S(1)} %bitcast.314, f32[512,12]{0,1:T(8,128)S(1)} %bitcast.316, pred[512,512]{0,1:T(8,128)(4,1)S(1)} %broadcast_compare_fusion.5, bf16[512,12,64]{0,2,1:T(8,128)(2,1)} %bitcast.291, bf16[1,512,12,64]{1,3,2,0:T(8,128)(2,1)} %copy-done.26), kind=kOutput, calls=%fused_computation.45.clone.1 | convolution fusion | flops 424673280 | bytes 20758528 | tf_op jit(solution)/shard_map/while/body/eval_jaxpr/sqhd,skhd->sqhk/dot_general | solution.py:273
  354.2 4.1 bitcast_add_fusion.8
  359.6 2.0 convolution_multiply_fusion.2
  362.5 1.6 copy-done.24
  365.8 2.2 constant_dynamic-slice_fusion.11
  368.9 3.0 fusion.154
  371.9 5.1 fusion.157
  377.0 8.4 %fusion.156 = bf16[512,12,512]{0,2,1:T(8,128)(2,1)} fusion(f32[12,512,512]{2,1,0:T(8,128)S(1)} %fusion.154, f32[512,12]{0,1:T(8,128)S(1)} %bitcast.314, f32[512,12]{0,1:T(8,128)S(1)} %bitcast.316, pred[512,512]{0,1:T(8,128)(4,1)S(1)} %broadcast_compare_fusion.5, bf16[512,12,64]{0,2,1:T(8,128)(2,1)} %bitcast.291, bf16[1,512,12,64]{1,3,2,0:T(8,128)(2,1)} %copy-done.26), kind=kOutput, calls=%fused_computation.45.clone.1 | convolution fusion | flops 424673280 | bytes 20758528 | tf_op jit(solution)/shard_map/while/body/eval_jaxpr/sqhd,skhd->sqhk/dot_general | solution.py:273
  385.4 4.1 bitcast_add_fusion.8
  390.2 2.0 convolution_multiply_fusion.2
  393.2 1.6 copy-done.24
  394.9 18.3 %reduce-scatter.12.cloned.1.call-done = bf16[24,3072]{1,0:T(8,128)(2,1)} async-done(((bf16[768,3072]{1,0:T(8,128)(2,1)}), bf16[24,3072]{1,0:T(8,128)(2,1)}) %reduce-scatter.12.cloned.1.call-update) | async-done | bytes 147472 | tf_op jit(solution)/shard_map/reduce_scatter | solution.py:358
  413.2 112.4 %reduce-scatter.14.cloned.1.call-done = bf16[96,768]{1,0:T(8,128)(2,1)} async-done(((bf16[3072,768]{1,0:T(8,128)(2,1)}), bf16[96,768]{1,0:T(8,128)(2,1)}) %reduce-scatter.14.cloned.1.call-update) | async-done | bytes 147472 | tf_op jit(solution)/shard_map/reduce_scatter | solution.py:358
  529.2 1.8 convolution_convert_fusion.3
  531.0 9.4 %reduce-scatter.6.cloned.1.call-done = bf16[1,1,512,1536]{2,3,1,0:T(8,128)(2,1)} async-done(((bf16[2,1,512,1536]{2,3,1,0:T(8,128)(2,1)}), bf16[1,1,512,1536]{2,3,1,0:T(8,128)(2,1)}) %reduce-scatter.6.cloned.1.call-update) | async-done | bytes 1572880 | tf_op jit(solution)/shard_map/reduce_scatter | solution.py:334
  540.4 6.0 fusion.67
  546.6 1.8 fusion.77
  548.9 2.7 fusion.70
  551.6 5.6 convolution_convert_fusion.2
  557.9 9.8 %fusion.73 = bf16[1,512,768]{2,1,0:T(8,128)(2,1)} fusion(f32[512,768]{1,0:T(8,128)} %copy-done.19, bf16[3072,768]{1,0:T(8,128)(2,1)} %all-gather.19.cloned.1.call-done, f32[768]{0:T(1024)S(1)} %reshape.612, f32[512,3072]{1,0:T(8,128)} %fusion.91, f32[3072]{0:T(1024)S(1)} %reshape.611), kind=kOutput, calls=%fused_computation.135 | convolution fusion | flops 2432827392 | bytes 13384704 | tf_op jit(solution)/shard_map/dot_general | solution.py:214
  567.7 1.4 fusion.74
  569.2 2.9 convert_element_type.251
  572.1 21.3 %all-gather.23.cloned.1.call-done = bf16[768,768]{1,0:T(8,128)(2,1)} async-done(((bf16[96,768]{1,0:T(8,128)(2,1)}), bf16[768,768]{1,0:T(8,128)(2,1)}) %all-gather.23.cloned.1.call-update) | async-done | bytes 1179664 | tf_op jit(solution)/shard_map/all_gather | solution.py:361
  593.4 2.8 convert_element_type.253
  596.3 97.9 %reduce-scatter.10.cloned.1.call-done = bf16[1,32,768]{2,1,0:T(8,128)(2,1)} async-done(((bf16[32,32,768]{2,1,0:T(8,128)(2,1)}), bf16[1,32,768]{2,1,0:T(8,128)(2,1)}) %reduce-scatter.10.cloned.1.call-update) | async-done | bytes 49168 | tf_op jit(solution)/shard_map/reduce_scatter | solution.py:358
  694.2 11.9 %all_gather.47 = bf16[8,32,768]{2,1,0:T(8,128)(2,1)S(1)} all-gather(bf16[1,32,768]{2,1,0:T(8,128)(2,1)} %reduce-scatter.10.cloned.1.call-done), channel_id=1, replica_groups=mesh['dp'=4,'fsdp'=4,'ctx'=2] {'dp','ctx'}, dimensions={0}, use_global_device_ids=true | all-gather | bytes 442368 | tf_op jit(solution)/shard_map/all_gather | solution.py:361
  709.1 93.4 %reduce-scatter.8.cloned.1.call-done = bf16[24,2304]{1,0:T(8,128)(2,1)} async-done(((bf16[768,2304]{1,0:T(8,128)(2,1)}), bf16[24,2304]{1,0:T(8,128)(2,1)}) %reduce-scatter.8.cloned.1.call-update) | async-done | bytes 110608 | tf_op jit(solution)/shard_map/reduce_scatter | solution.py:358
  802.5 13.1 %all_gather.46 = bf16[192,2304]{1,0:T(8,128)(2,1)S(1)} all-gather(bf16[24,2304]{1,0:T(8,128)(2,1)} %reduce-scatter.8.cloned.1.call-done), channel_id=1, replica_groups=mesh['dp'=4,'fsdp'=4,'ctx'=2] {'dp','ctx'}, dimensions={0}, use_global_device_ids=true | all-gather | bytes 995328 | tf_op jit(solution)/shard_map/all_gather | solution.py:361
  (238 shorter events, 36.6 us)
Async XLA Ops:
  7.2 76.2 %copy-start = (bf16[192,3072]{1,0:T(8,128)(2,1)S(1)}, bf16[192,3072]{1,0:T(8,128)(2,1)}, u32[]{:S(2)}) copy-start(bf16[192,3072]{1,0:T(8,128)(2,1)} %param.24) | copy-start | bytes 3538948
  7.2 65.4 %all-gather.13.cloned.1.call-start = ((), (), s32[]{:S(2)}) async-start(), calls=%async_computation.5 | async-start | bytes 3649536 | tf_op jit(solution)/shard_map/all_gather | solution.py:119
  8.9 80.2 %all-gather.27.cloned.1.call-start = ((), (), s32[]{:S(2)}) async-start(), calls=%async_computation.17 | async-start | bytes 2359296 | tf_op jit(solution)/shard_map/all_gather | solution.py:187
  26.3 50.8 %copy-start.36 = (f32[768]{0:T(1024)}, f32[768]{0:T(1024)S(1)}, u32[]{:S(2)}) copy-start(f32[768]{0:T(1024)S(1)} %reshape.606) | copy-start | bytes 9220
  26.4 50.7 %copy-start.41 = (f32[768]{0:T(1024)}, f32[768]{0:T(1024)S(1)}, u32[]{:S(2)}) copy-start(f32[768]{0:T(1024)S(1)} %reshape.607) | copy-start | bytes 9220
  27.7 49.3 %copy-start.33 = (f32[512]{0:T(512)}, f32[512]{0:T(512)S(1)}, u32[]{:S(2)}) copy-start(f32[512]{0:T(512)S(1)} %broadcast_multiply_fusion.5) | copy-start | bytes 6148
  29.2 47.8 %copy-start.38 = (f32[512]{0:T(512)}, f32[512]{0:T(512)S(1)}, u32[]{:S(2)}) copy-start(f32[512]{0:T(512)S(1)} %add_rsqrt_fusion.1) | copy-start | bytes 6148
  77.1 2.4 copy-start.22
  79.4 7.0 copy-start.32
  79.5 22.7 %all-gather.25.cloned.1.call-start = ((), (), s32[]{:S(2)}) async-start(), calls=%async_computation.16 | async-start | bytes 2359296 | tf_op jit(solution)/shard_map/all_gather | solution.py:186
  81.9 77.7 %all-gather.15.cloned.1.call-start = ((), (), s32[]{:S(2)}) async-start(), calls=%async_computation.6 | async-start | bytes 1216512 | tf_op jit(solution)/shard_map/all_gather | solution.py:119
  83.4 142.9 %all-gather.17.cloned.1.call-start = ((), (), s32[]{:S(2)}) async-start(), calls=%async_computation.7 | async-start | bytes 4866048 | tf_op jit(solution)/shard_map/all_gather | solution.py:119
  84.1 207.9 %all-gather.19.cloned.1.call-start = ((), (), s32[]{:S(2)}) async-start(), calls=%async_computation.8 | async-start | bytes 4866048 | tf_op jit(solution)/shard_map/all_gather | solution.py:119
  85.8 327.4 %reduce-scatter.12.cloned.1.call-start = ((), (), s32[]{:S(2)}) async-start(), calls=%async_computation.12 | async-start | bytes 4866048 | tf_op jit(solution)/shard_map/reduce_scatter | solution.py:358
  108.5 3.2 copy-start.17
  120.1 3.2 copy-start.17
  128.0 31.5 %copy-start.15 = (bf16[1,512,768]{2,1,0:T(8,128)(2,1)S(1)}, bf16[1,512,768]{2,1,0:T(8,128)(2,1)}, u32[]{:S(2)}) copy-start(bf16[1,512,768]{2,1,0:T(8,128)(2,1)} %param.19) | copy-start | bytes 2359300
  163.5 128.6 %copy-start.29 = (bf16[1,512,768]{2,1,0:T(8,128)(2,1)S(1)}, bf16[1,512,768]{2,1,0:T(8,128)(2,1)}, u32[]{:S(2)}) copy-start(bf16[1,512,768]{2,1,0:T(8,128)(2,1)} %param.20) | copy-start | bytes 2359300
  292.1 12.8 %copy-start.20 = (f32[512,768]{1,0:T(8,128)S(1)}, f32[512,768]{1,0:T(8,128)}, u32[]{:S(2)}) copy-start(f32[512,768]{1,0:T(8,128)} %copy-done.19) | copy-start | bytes 4718596
  303.2 1.7 copy-start.44
  309.8 215.8 %reduce-scatter.14.cloned.1.call-start = ((), (), s32[]{:S(2)}) async-start(), calls=%async_computation.14 | async-start | bytes 4866048 | tf_op jit(solution)/shard_map/reduce_scatter | solution.py:358
  309.9 6.9 copy-start.21
  316.8 1.8 copy-start.43
  321.7 1.8 copy-start.30
  332.5 207.9 %reduce-scatter.6.cloned.1.call-start = ((), (), s32[]{:S(2)}) async-start(), calls=%async_computation.9 | async-start | bytes 4718592 | tf_op jit(solution)/shard_map/reduce_scatter | solution.py:334
  332.8 3.9 copy-start.5
  332.8 3.9 copy-start.10
  345.7 8.4 %copy-start.3 = (bf16[1,512,768]{1,2,0:T(8,128)(2,1)S(1)}, bf16[1,512,768]{1,2,0:T(8,128)(2,1)}, u32[]{:S(2)}) copy-start(bf16[1,512,768]{1,2,0:T(8,128)(2,1)} %copy-done.2) | copy-start | bytes 2359300 | tf_op jit(solution)/shard_map/while
  345.7 8.4 %copy-start.7 = (f32[1,512,12,64]{1,3,2,0:T(8,128)S(1)}, f32[1,512,12,64]{1,3,2,0:T(8,128)}, u32[]{:S(2)}) copy-start(f32[1,512,12,64]{1,3,2,0:T(8,128)} %get-tuple-element.838) | copy-start | bytes 4718596 | tf_op jit(solution)/shard_map/while
  354.1 5.3 copy-start.4
  354.2 5.4 copy-start.6
  359.6 2.9 copy-start.8
  359.6 2.0 copy-start.12
  359.6 2.7 copy-start.23
  361.6 2.5 copy-start.11
  361.6 2.5 copy-start.27
  362.5 1.6 copy-start.24
  364.1 3.9 copy-start.5
  364.1 3.9 copy-start.10
  377.0 8.4 %copy-start.3 = (bf16[1,512,768]{1,2,0:T(8,128)(2,1)S(1)}, bf16[1,512,768]{1,2,0:T(8,128)(2,1)}, u32[]{:S(2)}) copy-start(bf16[1,512,768]{1,2,0:T(8,128)(2,1)} %copy-done.2) | copy-start | bytes 2359300 | tf_op jit(solution)/shard_map/while
  377.0 8.4 %copy-start.7 = (f32[1,512,12,64]{1,3,2,0:T(8,128)S(1)}, f32[1,512,12,64]{1,3,2,0:T(8,128)}, u32[]{:S(2)}) copy-start(f32[1,512,12,64]{1,3,2,0:T(8,128)} %get-tuple-element.838) | copy-start | bytes 4718596 | tf_op jit(solution)/shard_map/while
  385.4 4.6 copy-start.4
  385.4 4.8 copy-start.6
  390.2 2.9 copy-start.8
  390.2 2.0 copy-start.12
  390.2 2.7 copy-start.23
  392.2 2.5 copy-start.11
  392.3 2.5 copy-start.27
  393.2 1.6 copy-start.24
  394.8 132.7 %copy-start.40 = (bf16[3072]{0:T(1024)(128)(2,1)S(1)}, bf16[3072]{0:T(1024)(128)(2,1)}, u32[]{:S(2)}) copy-start(bf16[3072]{0:T(1024)(128)(2,1)} %get-tuple-element.634) | copy-start | bytes 18436
  394.8 133.0 %copy-start.9 = (f32[1,512,12,64]{1,3,2,0:T(8,128)S(1)}, f32[1,512,12,64]{1,3,2,0:T(8,128)}, u32[]{:S(2)}) copy-start(f32[1,512,12,64]{1,3,2,0:T(8,128)} %get-tuple-element.395) | copy-start | bytes 4718596
  394.8 133.9 %copy-start.14 = (f32[512,768]{1,0:T(8,128)S(1)}, f32[512,768]{1,0:T(8,128)}, u32[]{:S(2)}) copy-start(f32[512,768]{1,0:T(8,128)} %copy-done.13) | copy-start | bytes 4718596
  394.8 174.3 %all-gather.21.cloned.1.call-start = ((), (), s32[]{:S(2)}) async-start(), calls=%async_computation.13 | async-start | bytes 1327104 | tf_op jit(solution)/shard_map/all_gather | solution.py:361
  413.2 180.2 %all-gather.23.cloned.1.call-start = ((), (), s32[]{:S(2)}) async-start(), calls=%async_computation.15 | async-start | bytes 1327104 | tf_op jit(solution)/shard_map/all_gather | solution.py:361
  525.7 168.5 %reduce-scatter.10.cloned.1.call-start = ((), (), s32[]{:S(2)}) async-start(), calls=%async_computation.11 | async-start | bytes 1622016 | tf_op jit(solution)/shard_map/reduce_scatter | solution.py:358
  529.2 11.3 %copy-start.16 = (bf16[1,512,768]{2,1,0:T(8,128)(2,1)S(1)}, bf16[1,512,768]{2,1,0:T(8,128)(2,1)}, u32[]{:S(2)}) copy-start(bf16[1,512,768]{2,1,0:T(8,128)(2,1)} %param.19) | copy-start | bytes 2359300
  529.2 11.3 %copy-start.28 = (bf16[1,512,12,64]{1,3,2,0:T(8,128)(2,1)S(1)}, bf16[1,512,12,64]{1,3,2,0:T(8,128)(2,1)}, u32[]{:S(2)}) copy-start(bf16[1,512,12,64]{1,3,2,0:T(8,128)(2,1)} %convert.53) | copy-start | bytes 2359300
  529.2 11.3 %copy-start.34 = (f32[512]{0:T(512)S(1)}, f32[512]{0:T(512)}, u32[]{:S(2)}) copy-start(f32[512]{0:T(512)} %copy-done.33) | copy-start | bytes 6148
  529.2 11.3 %copy-start.37 = (f32[768]{0:T(1024)S(1)}, f32[768]{0:T(1024)}, u32[]{:S(2)}) copy-start(f32[768]{0:T(1024)} %copy-done.36) | copy-start | bytes 9220
  529.2 11.3 %copy-start.39 = (f32[512]{0:T(512)S(1)}, f32[512]{0:T(512)}, u32[]{:S(2)}) copy-start(f32[512]{0:T(512)} %copy-done.38) | copy-start | bytes 6148
  548.4 3.2 copy-start.42
  551.5 251.0 %reduce-scatter.8.cloned.1.call-start = ((), (), s32[]{:S(2)}) async-start(), calls=%async_computation.10 | async-start | bytes 3649536 | tf_op jit(solution)/shard_map/reduce_scatter | solution.py:358
  557.9 9.8 %copy-start.31 = (f32[512,768]{1,0:T(8,128)S(1)}, f32[512,768]{1,0:T(8,128)}, u32[]{:S(2)}) copy-start(f32[512,768]{1,0:T(8,128)} %get-tuple-element.633) | copy-start | bytes 4718596
  706.1 110.8 %copy-start.1 = (bf16[192,3072]{1,0:T(8,128)(2,1)S(1)}, bf16[192,3072]{1,0:T(8,128)(2,1)}, u32[]{:S(2)}) copy-start(bf16[192,3072]{1,0:T(8,128)(2,1)} %param.24) | copy-start | bytes 3538948
  (10 other events, 11.4 us)
Sparse Core Ops, SparseCore 0:
  11.5 61.0 all-gather.12
  79.6 9.4 all-gather.26
  91.2 10.9 all-gather.24
  105.5 54.0 all-gather.14
  162.3 63.9 all-gather.16
  229.6 62.4 all-gather.18
  309.9 103.1 reduce-scatter.11
  419.5 106.0 reduce-scatter.13
  527.9 12.4 reduce-scatter.5
  542.3 24.9 all-gather.20
  569.3 24.0 all-gather.22
  599.4 94.7 reduce-scatter.9
  700.5 101.9 reduce-scatter.7

commit v2 on v1

--- a/solution.py
+++ b/solution.py
@@ -3,6 +3,8 @@
 import jax
 import jax.numpy as jnp
 from jax import lax
+from jax.experimental import pallas as pl
+from jax.experimental.pallas import tpu as pltpu
 from jax.sharding import PartitionSpec as P
 
 HEADS = 12
@@ -84,6 +86,277 @@
         return (new_max, row_total, weighted)
 
     return lax.fori_loop(0, block_count, one_block, state_now)
+
+
+TILE = 16
+MESH_ID = pl.DeviceIdType.MESH
+
+
+def peer_table():
+    dp, z, core = lax.axis_index("dp"), lax.axis_index("fsdp"), lax.axis_index("ctx")
+    row, col = dp // 2, dp % 2
+    sibling = {"ctx": 1 - core}
+    beside = {"dp": row * 2 + (1 - col)}
+    above = {"dp": (1 - row) * 2 + col}
+    across = {"dp": (1 - row) * 2 + (1 - col)}
+    return row, col, z, core, sibling, beside, above, across
+
+
+def greet(peers):
+    barrier = pltpu.get_barrier_semaphore()
+    for peer in peers:
+        pl.semaphore_signal(barrier, inc=1, device_id=peer, device_id_type=MESH_ID)
+    pl.semaphore_wait(barrier, len(peers))
+
+
+def push(source, target, sems, slot, peer):
+    return pltpu.make_async_remote_copy(
+        src_ref=source,
+        dst_ref=target,
+        send_sem=sems.at[0, slot],
+        recv_sem=sems.at[1, slot],
+        device_id=peer,
+        device_id_type=MESH_ID,
+    )
+
+
+def gather_kernel(own, whole, line_sems, plane_sems, pair_sems, local_sem):
+    row, col, z, core, sibling, beside, above, across = peer_table()
+    line_peers = [{"fsdp": lax.rem(z + 4 - k, 4)} for k in (1, 2, 3)]
+    greet([sibling, beside, above, across] + line_peers)
+    keep = pltpu.make_async_copy(own, whole.at[z], local_sem)
+    keep.start()
+    line = [
+        push(own.at[core, row, col], whole.at[z, core, row, col], line_sems, k, line_peers[k])
+        for k in (0, 2, 1)
+    ]
+    for copy in line:
+        copy.start()
+    plane = []
+    origins = [lax.rem(z + 1 + k, 4) for k in (0, 2, 1)]
+    for step, origin in enumerate(origins):
+        line[step].wait_recv()
+        piece = whole.at[origin, core, row, col]
+        plane.append(
+            [
+                push(piece, piece, plane_sems, step * 3 + index, peer)
+                for index, peer in enumerate((beside, above, across))
+            ]
+        )
+        for copy in plane[-1]:
+            copy.start()
+    pair = []
+    for step, origin in enumerate(origins):
+        for copy in plane[step]:
+            copy.wait_recv()
+        half = whole.at[origin, core]
+        pair.append(push(half, half, pair_sems, step, sibling))
+        pair[-1].start()
+    for copy in pair:
+        copy.wait()
+    for copies in plane:
+        for copy in copies:
+            copy.wait_send()
+    for copy in line:
+        copy.wait_send()
+    keep.wait()
+
+
+def gather_bundle(own):
+    rows, width = own.shape[-2:]
+    return pl.pallas_call(
+        gather_kernel,
+        out_shape=jax.ShapeDtypeStruct((4, 2, 2, 2, rows, width), own.dtype),
+        in_specs=[pl.BlockSpec(memory_space=pl.ANY)],
+        out_specs=pl.BlockSpec(memory_space=pl.ANY),
+        scratch_shapes=[
+            pltpu.SemaphoreType.DMA((2, 3)),
+            pltpu.SemaphoreType.DMA((2, 9)),
+            pltpu.SemaphoreType.DMA((2, 3)),
+            pltpu.SemaphoreType.DMA,
+        ],
+        compiler_params=pltpu.CompilerParams(collective_id=1, has_side_effects=True),
+        name="gather_weights",
+    )(own)
+
+
+def add_rows(target, target_at, source, source_at, start, count, source_start):
+    @pl.loop(0, count // TILE)
+    def _(step):
+        offset = pl.multiple_of(step * TILE, TILE)
+        here = target_at + (pl.ds(start + offset, TILE),)
+        there = source_at + (pl.ds(source_start + offset, TILE),)
+        target[here] = (
+            target[here].astype(jnp.float32) + source[there].astype(jnp.float32)
+        ).astype(target.dtype)
+
+
+def sum_kernel(
+    grads,
+    shared,
+    held,
+    from_pair,
+    from_beside,
+    from_above,
+    late_beside,
+    late_above,
+    from_line,
+    done,
+    load_sems,
+    pair_sems,
+    beside_sems,
+    above_sems,
+    late_beside_sems,
+    late_above_sems,
+    line_sems,
+    plane_sems,
+    last_sems,
+    local_sem,
+):
+    row, col, z, core, sibling, beside, above, across = peer_table()
+    rows = grads.shape[-2]
+    cut = (rows // 2 + TILE - 1) // TILE * TILE
+    tail = rows - cut
+    order = [lax.rem(z + 1 + k, 4) for k in range(4)]
+    line_peers = [{"fsdp": order[k]} for k in range(3)]
+    greet([sibling, beside, above, across] + line_peers)
+    loads, pairs = [], []
+    for k in range(4):
+        pairs.append(push(grads.at[order[k], 1 - core], from_pair.at[k], pair_sems, k, sibling))
+        pairs[-1].start()
+        loads.append(pltpu.make_async_copy(grads.at[order[k], core], held.at[k], load_sems.at[k]))
+        loads[-1].start()
+    first = []
+    for k in range(4):
+        loads[k].wait()
+        pairs[k].wait_recv()
+        for r in range(2):
+            for c in range(2):
+                add_rows(held, (k, r, c), from_pair, (k, r, c), 0, rows, 0)
+        first.append(
+            (
+                push(
+                    held.at[k, :, 1 - col, pl.ds(0, cut)],
+                    from_beside.at[k],
+                    beside_sems,
+                    k,
+                    beside,
+                ),
+                push(
+                    held.at[k, 1 - row, :, pl.ds(cut, tail)],
+                    from_above.at[k],
+                    above_sems,
+                    k,
+                    above,
+                ),
+            )
+        )
+        for copy in first[-1]:
+            copy.start()
+    second = []
+    for k in range(4):
+        for copy in first[k]:
+            copy.wait_recv()
+        for other in range(2):
+            add_rows(held, (k, other, col), from_beside, (k, other), 0, cut, 0)
+            add_rows(held, (k, row, other), from_above, (k, other), cut, tail, 0)
+        second.append(
+            (
+                push(
+                    held.at[k, 1 - row, col, pl.ds(0, cut)],
+                    late_above.at[k],
+                    late_above_sems,
+                    k,
+                    above,
+                ),
+                push(
+                    held.at[k, row, 1 - col, pl.ds(cut, tail)],
+                    late_beside.at[k],
+                    late_beside_sems,
+                    k,
+                    beside,
+                ),
+            )
+        )
+        for copy in second[-1]:
+            copy.start()
+    line = []
+    for k in range(4):
+        for copy in second[k]:
+            copy.wait_recv()
+        add_rows(held, (k, row, col), late_above, (k,), 0, cut, 0)
+        add_rows(held, (k, row, col), late_beside, (k,), cut, tail, 0)
+        if k < 3:
+            line.append(push(held.at[k, row, col], from_line.at[k], line_sems, k, line_peers[k]))
+            line[-1].start()
+    for copy in line:
+        copy.wait_recv()
+
+    @pl.loop(0, rows // TILE)
+    def _(step):
+        here = pl.ds(pl.multiple_of(step * TILE, TILE), TILE)
+        total = held[3, row, col, here].astype(jnp.float32)
+        for k in range(3):
+            total = total + from_line[k, here].astype(jnp.float32)
+        done[core, row, col, here] = total.astype(done.dtype)
+
+    piece = done.at[core, row, col]
+    plane = [
+        push(piece, piece, plane_sems, index, peer)
+        for index, peer in enumerate((beside, above, across))
+    ]
+    for copy in plane:
+        copy.start()
+    for copy in plane:
+        copy.wait_recv()
+    last = push(done.at[core], done.at[core], last_sems, 0, sibling)
+    last.start()
+    for copies in first + second:
+        for copy in copies:
+            copy.wait_send()
+    for copy in pairs + line + plane:
+        copy.wait_send()
+    last.wait()
+    out = pltpu.make_async_copy(done, shared, local_sem)
+    out.start()
+    out.wait()
+
+
+def sum_bundle(grads):
+    rows, width = grads.shape[-2:]
+    kind = grads.dtype
+    cut = (rows // 2 + TILE - 1) // TILE * TILE
+    tail = rows - cut
+    return pl.pallas_call(
+        sum_kernel,
+        out_shape=jax.ShapeDtypeStruct((2, 2, 2, rows, width), kind),
+        in_specs=[pl.BlockSpec(memory_space=pl.ANY)],
+        out_specs=pl.BlockSpec(memory_space=pl.ANY),
+        scratch_shapes=[
+            pltpu.VMEM((4, 2, 2, rows, width), kind),
+            pltpu.VMEM((4, 2, 2, rows, width), kind),
+            pltpu.VMEM((4, 2, cut, width), kind),
+            pltpu.VMEM((4, 2, tail, width), kind),
+            pltpu.VMEM((4, tail, width), kind),
+            pltpu.VMEM((4, cut, width), kind),
+            pltpu.VMEM((3, rows, width), kind),
+            pltpu.VMEM((2, 2, 2, rows, width), kind),
+            pltpu.SemaphoreType.DMA((4,)),
+            pltpu.SemaphoreType.DMA((2, 4)),
+            pltpu.SemaphoreType.DMA((2, 4)),
+            pltpu.SemaphoreType.DMA((2, 4)),
+            pltpu.SemaphoreType.DMA((2, 4)),
+            pltpu.SemaphoreType.DMA((2, 4)),
+            pltpu.SemaphoreType.DMA((2, 3)),
+            pltpu.SemaphoreType.DMA((2, 3)),
+            pltpu.SemaphoreType.DMA((2, 1)),
+            pltpu.SemaphoreType.DMA,
+        ],
+        compiler_params=pltpu.CompilerParams(
+            collective_id=2, has_side_effects=True, vmem_limit_bytes=48 * 1024 * 1024
+        ),
+        name="sum_gradients",
+    )(grads)
 
 
 def body(
@@ -131,8 +404,52 @@
             norm2_shift,
         ]
     )
-    small_rows = lax.all_gather(small_row, "fsdp", axis=0, tiled=False)
     part = model_width // shards
+    fits = (lax.axis_size("dp"), shards, lax.axis_size("ctx")) == (4, 4, 2)
+    widths = [w_qkv.shape[1], w_out.shape[1], w_up.shape[1], w_down.shape[1]]
+    depths = [w.shape[0] // copies for w in (w_qkv, w_out, w_up, w_down)]
+    small_lines = small_row.shape[0] // model_width
+    spare = -small_lines % TILE
+
+    def stack_rows(matrices, small):
+        groups = small.shape[0]
+        parts = [
+            m.reshape(groups, copies, rows, width // model_width, model_width)
+            .swapaxes(2, 3)
+            .reshape(groups, copies, -1, model_width)
+            for m, rows, width in zip(matrices, depths, widths)
+        ]
+        lines = small.reshape(groups, 1, small_lines, model_width)
+        parts.append(jnp.pad(lines, ((0, 0), (0, copies - 1), (0, spare), (0, 0))))
+        return jnp.concatenate(parts, axis=2).reshape(groups, 2, 2, 2, -1, model_width)
+
+    def unstack_rows(bundle):
+        groups = bundle.shape[0]
+        bundle = bundle.reshape(groups, copies, -1, model_width)
+        found, start = [], 0
+        for rows, width in zip(depths, widths):
+            blocks = []
+            for _ in range(width // model_width):
+                blocks.append(bundle[:, :, start : start + rows].reshape(-1, model_width))
+                start += rows
+            found.append(blocks)
+        small = bundle[:, 0, start : start + small_lines].reshape(groups, -1)
+        return found, small
+
+    if fits:
+        (qkv_blocks, out_blocks, up_blocks, down_blocks), small_rows = unstack_rows(
+            gather_bundle(stack_rows((w_qkv, w_out, w_up, w_down), small_row[None])[0])
+        )
+        whole_qkv = jnp.concatenate(qkv_blocks, axis=1)
+        whole_out = out_blocks[0]
+        whole_up = jnp.concatenate(up_blocks, axis=1)
+        whole_down = down_blocks[0]
+    else:
+        small_rows = lax.all_gather(small_row, "fsdp", axis=0, tiled=False)
+        whole_qkv = gather_whole(w_qkv)
+        whole_out = gather_whole(w_out)
+        whole_up = gather_whole(w_up)
+        whole_down = gather_whole(w_down)
 
     def small_part(start, width):
         return small_rows[:, start : start + width].reshape(-1)
@@ -147,10 +464,6 @@
     shift_one = small_part(rest + 2 * part, part)
     gain_two = small_part(rest + 3 * part, part)
     shift_two = small_part(rest + 4 * part, part)
-    whole_qkv = gather_whole(w_qkv)
-    whole_out = gather_whole(w_out)
-    whole_up = gather_whole(w_up)
-    whole_down = gather_whole(w_down)
     flat_in = inputs.reshape(row_count, model_width).astype(jnp.float32)
     normed_one, scale_one = normalize(flat_in)
     hidden_one = (normed_one * gain_one.astype(jnp.float32) + shift_one.astype(jnp.float32)).astype(
@@ -375,24 +688,35 @@
         axis=1,
     )
     small_width = small_grads.shape[1]
-    piece_width = small_width // copies
-    out_rows = model_width // (shards * copies)
-    packed = jnp.concatenate(
-        [
-            grad_out.astype(jnp.bfloat16).reshape(shards * copies, out_rows, model_width),
-            jnp.pad(
-                small_grads.astype(jnp.bfloat16).reshape(shards * copies, 1, piece_width),
-                ((0, 0), (0, 7), (0, model_width - piece_width)),
-            ),
-        ],
-        axis=1,
-    )
-    own_down = share(grad_down)
-    own_up = share(grad_up)
-    own_qkv = share(grad_qkv_w)
-    own_packed = share(packed)
-    own_out = own_packed[:, :out_rows].reshape(copies * out_rows, model_width)
-    own_small = own_packed[:, out_rows, :piece_width].reshape(small_width)
+    if fits:
+        grads = [g.astype(jnp.bfloat16) for g in (grad_qkv_w, grad_out, grad_up, grad_down)]
+        found, own_small = unstack_rows(
+            sum_bundle(stack_rows(grads, small_grads.astype(jnp.bfloat16)))[None]
+        )
+        own_qkv, own_out, own_up, own_down = (
+            jnp.concatenate([block.astype(jnp.float32) for block in blocks], axis=1)
+            for blocks in found
+        )
+        own_small = own_small.reshape(small_width).astype(jnp.float32)
+    else:
+        piece_width = small_width // copies
+        out_rows = model_width // (shards * copies)
+        packed = jnp.concatenate(
+            [
+                grad_out.astype(jnp.bfloat16).reshape(shards * copies, out_rows, model_width),
+                jnp.pad(
+                    small_grads.astype(jnp.bfloat16).reshape(shards * copies, 1, piece_width),
+                    ((0, 0), (0, 7), (0, model_width - piece_width)),
+                ),
+            ],
+            axis=1,
+        )
+        own_down = share(grad_down)
+        own_up = share(grad_up)
+        own_qkv = share(grad_qkv_w)
+        own_packed = share(packed)
+        own_out = own_packed[:, :out_rows].reshape(copies * out_rows, model_width)
+        own_small = own_packed[:, out_rows, :piece_width].reshape(small_width)
 
     def own_part(start, width):
         return own_small[start : start + width]

time: 829 us -> 534 us (0.64)
  waiting for transfers between devices: 559 us -> 13.3 us
  Pallas kernels: 0 us -> 243 us
  local copies, waits for them, and re-layouts: 48.7 us -> 116 us
  blocking collectives: 35.8 us -> 0 us
  matrix products: 128 us -> 110 us
    reduce_scatter x4 -> x0, waiting for transfers between devices: 322 us -> none  [share(): lax.psum_scatter(grad.astype(jnp.bfloat16), spread, scatter_dimension=0,...]
    pallas_call x0 -> x2, Pallas kernels: none -> 243 us  [the longest x1 126 us: sum_bundle(): pl.pallas_call(sum_kernel, out_shape=jax.ShapeDtypeStruct((2, 2, 2, rows,...]
    all_gather x6 -> x0, waiting for transfers between devices: 214 us -> none  [the longest x4 193 us: gather_whole(): return lax.all_gather(own_piece(shard), spread, axis=0, tiled=True)]
    all_gather x3 -> x0, blocking collectives: 35.8 us -> none  [the longest x2 25 us: share(): lax.all_gather(piece, ('dp', 'ctx'), axis=0, tiled=True).astype(jnp.float32)]
    reshape x0 -> x6, local copies, waits for them, and re-layouts: none -> 27.5 us  [stack_rows(): m.reshape(groups, copies, rows, width // model_width, model_width)]
    slice x2 -> x5, local copies, waits for them, and re-layouts: 0.89 us -> 16.6 us  [the longest x4 15.8 us: unstack_rows(): blocks.append(bundle[:, :, start:start + rows].reshape(-1, model_width))]
    unnamed x62 -> x146, local copies, waits for them, and re-layouts: 10.3 us -> 24.5 us
    reduce_scatter x1, waiting for transfers between devices: 9.42 us -> 0.01 us  [body(): lax.psum_scatter(key_terms.astype(jnp.bfloat16), 'ctx', scatter_dimension...]
  transfers between devices with their start and end apart: 13 -> 3, of which waited for: 12 -> 2; matrix products, arithmetic and copies ran while one was open for 21% -> 10% of each run, Pallas kernels for 0% -> 0%
where the time goes in v2:
time: 534 us; the launch traced here: 529 us
  Pallas kernels  243 us (46%)
  local copies, waits for them, and re-layouts  116 us (22%)
  matrix products  110 us (21%)
  other arithmetic  28.5 us (5%)
  between operations  14.9 us (3%)
  waiting for transfers between devices  13.3 us (2%)
    pallas_call x1, Pallas kernels, sum_bundle(): pl.pallas_call(sum_kernel, out_shape=jax.ShapeDtypeStruct((2, 2, 2, rows,...  126 us
    pallas_call x1, Pallas kernels, gather_bundle(): pl.pallas_call(gather_kernel, out_shape=jax.ShapeDtypeStruct((4, 2, 2, 2,...  117 us
    reshape x6, local copies, waits for them, and re-layouts, stack_rows(): m.reshape(groups, copies, rows, width // model_width, model_width)  27.5 us
    unnamed x146, local copies, waits for them, and re-layouts  24.5 us
    dot_general x2, matrix products, score_grads(): jnp.einsum('sqhd,skhd->sqhk', grad_block, value_block, preferred_element_...  16.8 us
    slice x4, local copies, waits for them, and re-layouts, unstack_rows(): blocks.append(bundle[:, :, start:start + rows].reshape(-1, model_width))  15.8 us
    all_gather x1, waiting for transfers between devices, body(): lax.all_gather(key_rows, 'ctx', axis=1, tiled=True)  11.4 us
  transfers between devices with their start and end apart: 3, of which 2 were waited for; matrix products, arithmetic and copies ran while one was open for 10% of the time, Pallas kernels for 0%

profile of v2, /device:TPU:9, one launch (start us, length us, event | category | flops | bytes accessed | tf_op | source)
XLA Modules:
  0.0 528.6 jit_solution(6557739399681408984)
XLA Ops:
  8.1 4.8 concatenate.67
  12.9 2.2 reshape.679
  21.1 116.8 %gather_weights.1 = bf16[4,2,2,2,304,768]{5,4,3,2,1,0:T(8,128)(2,1)} custom-call(bf16[2,2,2,304,768]{4,3,2,1,0:T(8,128)(2,1)} %constant_dynamic-update-slice_fusion.own), custom_call_target="tpu_custom_call" | custom-call | tf_op jit(solution)/shard_map/gather_weights/pallas_call | solution.py:167
  138.7 6.7 %fusion.94 = (bf16[4,8,24,768]{3,2,1,0:T(8,128)(2,1)}, bf16[4,8,24,768]{3,2,1,0:T(8,128)(2,1)}, bf16[4,8,24,768]{3,2,1,0:T(8,128)(2,1)}, bf16[4,8,24,768]{3,2,1,...) fusion(bf16[4,8,304,768]{3,2,1,0:T(8,128)(2,1)} %bitcast.326), kind=kLoop, calls=%fused_computation.201 | loop fusion | bytes 18874368 | tf_op jit(solution)/shard_map/slice | solution.py:433
  147.2 3.4 fusion.72
  150.7 2.1 copy-done.21
  153.9 2.4 slice.263
  156.7 4.8 slice.222
  162.2 1.8 all-gather.7.cloned.1.call-done
  164.0 1.7 copy.70
  165.7 11.4 %all-gather.5.cloned.1.call-done = bf16[1024,768]{1,0:T(8,128)(2,1)} async-done(((bf16[512,768]{1,0:T(8,128)(2,1)}), bf16[1024,768]{1,0:T(8,128)(2,1)}) %all-gather.5.cloned.1.call-update) | async-done | bytes 1572880 | tf_op jit(solution)/shard_map/all_gather | solution.py:499
  177.1 2.6 copy.69
  179.7 23.3 %while.35 = (s32[]{:T(128)}, f32[1,512,12]{1,2,0:T(8,128)S(1)}, f32[1,512,12]{1,2,0:T(8,128)S(1)}, f32[1,512,12,64]{1,3,2,0:T(8,128)}, s32[4]{0:T(128)S(1)}, /*i...) while((s32[]{:T(128)}, f32[1,512,12]{1,2,0:T(8,128)S(1)}, ...), condition=%wide.region_7.8_spmd.clone, body=%wide.region_3.7_spmd.clone.sunk | while | flops 847700480 | bytes 60438800 | solution.py:88
  181.3 2.1 fusion.141
  183.4 3.1 fusion.143
  186.6 3.6 bitcast_add_fusion.7
  193.0 2.1 fusion.141
  195.1 3.1 fusion.143
  198.2 3.6 bitcast_add_fusion.7
  203.0 1.8 fusion.80
  204.8 2.5 fusion.98
  207.8 2.7 fusion.75
  210.5 8.1 %fusion.99 = (bf16[3072]{0:T(1024)(128)(2,1)S(1)}, bf16[512,3072]{1,0:T(8,128)(2,1)S(1)}) fusion(bf16[3072,768]{1,0:T(8,128)(2,1)S(1)} %bitcast.342, bf16[1,512,768]{2,1,0:T(8,128)(2,1)S(1)} %copy-done.30, f32[512,3072]{1,0:T(8,128)S(1)} %fusion.75, f32[3072]{0:T(1024)S(1)} %reshape.714), kind=kOutput, calls=%fused_computation.206 | convolution fusion | flops 2456810496 | bytes 14960640 | tf_op jit(solution)/shard_map/rd,fd->rf/dot_general | solution.py:535
  218.6 3.0 multiply_reduce_fusion
  223.5 1.7 convolution_convert_fusion.4
  225.2 1.4 copy.71
  226.7 1.7 multiply_reduce_fusion.1
  228.4 61.2 %while.36 = (s32[]{:T(128)}, f32[1,512,12,64]{1,3,2,0:T(8,128)}, bf16[2,1,512,1536]{2,3,1,0:T(8,128)(2,1)}, s32[2]{0:T(128)S(1)}, bf16[1,1024,768]{1,2,0:T(8,128...) while((s32[]{:T(128)}, f32[1,512,12,64]{1,3,2,0:T(8,128)}, ...), condition=%wide.region_15.16_spmd.clone, body=%wide.region_13.15_spmd.clone.sunk | while | flops 2056409600 | bytes 171530928 | solution.py:644
  230.2 2.2 constant_dynamic-slice_fusion.7
  233.3 3.0 fusion.154
  236.2 5.1 fusion.157
  241.3 8.4 %fusion.156 = bf16[512,12,512]{0,2,1:T(8,128)(2,1)} fusion(f32[12,512,512]{2,1,0:T(8,128)S(1)} %fusion.154, f32[512,12]{0,1:T(8,128)S(1)} %bitcast.397, f32[512,12]{0,1:T(8,128)S(1)} %bitcast.399, pred[512,512]{0,1:T(8,128)(4,1)S(1)} %broadcast_compare_fusion.5, bf16[512,12,64]{0,2,1:T(8,128)(2,1)} %bitcast.330, bf16[1,512,12,64]{1,3,2,0:T(8,128)(2,1)} %copy-done.27), kind=kOutput, calls=%fused_computation.45.clone.1 | convolution fusion | flops 424673280 | bytes 20758528 | tf_op jit(solution)/shard_map/while/body/eval_jaxpr/sqhd,skhd->sqhk/dot_general | solution.py:586
  249.7 4.1 bitcast_add_fusion.8
  254.5 2.0 convolution_multiply_fusion.2
  257.4 1.6 copy-done.23
  260.7 2.2 constant_dynamic-slice_fusion.7
  263.8 3.0 fusion.154
  266.8 5.1 fusion.157
  271.9 8.4 %fusion.156 = bf16[512,12,512]{0,2,1:T(8,128)(2,1)} fusion(f32[12,512,512]{2,1,0:T(8,128)S(1)} %fusion.154, f32[512,12]{0,1:T(8,128)S(1)} %bitcast.397, f32[512,12]{0,1:T(8,128)S(1)} %bitcast.399, pred[512,512]{0,1:T(8,128)(4,1)S(1)} %broadcast_compare_fusion.5, bf16[512,12,64]{0,2,1:T(8,128)(2,1)} %bitcast.330, bf16[1,512,12,64]{1,3,2,0:T(8,128)(2,1)} %copy-done.27), kind=kOutput, calls=%fused_computation.45.clone.1 | convolution fusion | flops 424673280 | bytes 20758528 | tf_op jit(solution)/shard_map/while/body/eval_jaxpr/sqhd,skhd->sqhk/dot_general | solution.py:586
  280.3 4.1 bitcast_add_fusion.8
  285.1 2.0 convolution_multiply_fusion.2
  287.9 1.6 copy-done.23
  294.2 6.4 %convolution_convert_fusion.1 = bf16[768,3072]{1,0:T(8,128)(2,1)} fusion(bf16[512,3072]{1,0:T(8,128)(2,1)} %copy-done.71, f32[512,768]{1,0:T(8,128)S(1)} %copy-done.19, f32[768]{0:T(1024)S(1)} %copy-done.67, f32[768]{0:T(1024)S(1)} %reshape.712, f32[512]{0:T(512)S(1)} %add_rsqrt_fusion, f32[512]{0:T(512)S(1)} %broadcast_multiply_fusion.4), kind=kOutput, calls=%fused_computation.92 | convolution fusion | flops 2420244480 | bytes 9447424 | tf_op jit(solution)/shard_map/rd,rf->df/dot_general | solution.py:538
  300.6 9.9 %reshape.701 = bf16[4,8,24,4,768]{4,3,2,1,0:T(4,128)(2,1)} reshape(bf16[768,3072]{1,0:T(8,128)(2,1)} %convolution_convert_fusion.1) | data formatting | bytes 9437184 | tf_op jit(solution)/shard_map/reshape | solution.py:417
  310.6 5.6 %copy.75 = bf16[4,8,24,4,768]{4,2,3,1,0:T(8,128)(2,1)} copy(bf16[4,8,24,4,768]{4,3,2,1,0:T(4,128)(2,1)} %reshape.701) | data formatting | bytes 9437184 | tf_op jit(solution)/shard_map/reshape | solution.py:417
  318.0 9.1 %convolution_convert_fusion = bf16[3072,768]{1,0:T(8,128)(2,1)} fusion(bf16[1,512,768]{2,1,0:T(8,128)(2,1)S(1)} %copy-done.32, f32[512,3072]{1,0:T(8,128)} %copy-done.72, f32[3072]{0:T(1024)S(1)} %copy-done.59), kind=kOutput, calls=%fused_computation.91 | convolution fusion | flops 2434007040 | bytes 11808768 | tf_op jit(solution)/shard_map/rf,rd->fd/dot_general | solution.py:533
  327.2 4.9 fusion.73
  332.1 7.0 %fusion.66 = (bf16[768]{0:T(1024)(128)(2,1)}, f32[512]{0:T(512)}, f32[512]{0:T(512)}, bf16[768]{0:T(1024)(128)(2,1)}, f32[512,768]{1,0:T(8,128)}) fusion(bf16[1,512,768]{2,1,0:T(8,128)(2,1)S(1)} %copy-done.15, f32[512]{0:T(512)} %copy-done.60, f32[512]{0:T(512)S(1)} %copy-done.54, f32[768]{0:T(1024)S(1)} %copy-done.57, bf16[768,768]{1,0:T(8,128)(2,1)} %bitcast.368, ...), kind=kOutput, calls=%fused_computation.114 | convolution fusion | flops 1831204352 | bytes 8271872 | tf_op jit(solution)/shard_map/re,de->rd/dot_general | solution.py:657
  340.1 4.4 convolution_convert_fusion.2
  351.2 1.5 concatenate.77
  354.3 8.7 %reshape.700 = bf16[4,8,24,3,768]{4,3,2,1,0:T(4,128)(2,1)} reshape(bf16[768,2304]{1,0:T(8,128)(2,1)} %convolution_convert_fusion.2) | data formatting | bytes 7077888 | tf_op jit(solution)/shard_map/reshape | solution.py:417
  363.0 3.0 copy.74
  366.0 2.1 constant_dynamic-update-slice_fusion.9
  370.0 2.5 constant_dynamic-update-slice_fusion.7
  372.5 2.6 constant_dynamic-update-slice_fusion.6
  376.0 126.1 %sum_gradients.1 = bf16[2,2,2,304,768]{4,3,2,1,0:T(8,128)(2,1)S(1)} custom-call(bf16[4,2,2,2,304,768]{5,4,3,2,1,0:T(8,128)(2,1)} %constant_dynamic-update-slice_fusion.5.grads), custom_call_target="tpu_custom_call" | custom-call | tf_op jit(solution)/shard_map/sum_gradients/pallas_call | solution.py:330
  502.2 1.8 copy-done
  505.3 1.4 slice.234
  506.7 3.0 fusion.95
  511.6 1.4 slice_convert_fusion.8
  513.0 1.8 bitcast_convert_fusion.1
  514.8 1.7 bitcast_convert_fusion
  516.5 2.3 fusion.76
  520.2 1.7 maximum_convert_fusion
  (307 shorter events, 49.4 us)
Async XLA Ops:
  7.2 8.0 %copy-start.49 = (bf16[192,3072]{1,0:T(8,128)(2,1)S(1)}, bf16[192,3072]{1,0:T(8,128)(2,1)}, u32[]{:S(2)}) copy-start(bf16[192,3072]{1,0:T(8,128)(2,1)} %param.24) | copy-start | bytes 3538948
  7.2 156.8 %all-gather.7.cloned.1.call-start = ((), (), s32[]{:S(2)}) async-start(), calls=%async_computation.3 | async-start | bytes 2359296 | tf_op jit(solution)/shard_map/all_gather | solution.py:500
  16.1 3.1 copy-start.50
  138.7 6.7 %copy-start.14 = (bf16[1,512,768]{2,1,0:T(8,128)(2,1)S(1)}, bf16[1,512,768]{2,1,0:T(8,128)(2,1)}, u32[]{:S(2)}) copy-start(bf16[1,512,768]{2,1,0:T(8,128)(2,1)} %param.19) | copy-start | bytes 2359300
  145.4 5.2 copy-start.35
  145.4 5.2 copy-start.36
  145.6 5.0 copy-start.53
  146.0 4.6 copy-start.60
  147.1 3.5 copy-start.56
  147.2 3.5 copy-start.64
  153.9 23.2 %all-gather.5.cloned.1.call-start = ((), (), s32[]{:S(2)}) async-start(), calls=%async_computation.2 | async-start | bytes 2359296 | tf_op jit(solution)/shard_map/all_gather | solution.py:499
  156.3 175.7 %reduce-scatter.2.cloned.1.call-start = ((), (), s32[]{:S(2)}) async-start(), calls=%async_computation.1 | async-start | bytes 4718592 | tf_op jit(solution)/shard_map/reduce_scatter | solution.py:647
  156.7 5.4 %copy-start.52 = (s32[4]{0:T(128)S(1)}, s32[4]{0:T(128)}, u32[]{:S(2)}) copy-start(s32[4]{0:T(128)} %param.21) | copy-start | bytes 52
  161.5 49.0 %copy-start.58 = (f32[3072]{0:T(1024)}, f32[3072]{0:T(1024)S(1)}, u32[]{:S(2)}) copy-start(f32[3072]{0:T(1024)S(1)} %reshape.714) | copy-start | bytes 36868
  161.7 46.0 %copy-start.66 = (f32[768]{0:T(1024)}, f32[768]{0:T(1024)S(1)}, u32[]{:S(2)}) copy-start(f32[768]{0:T(1024)S(1)} %reshape.713) | copy-start | bytes 9220
  183.4 3.2 copy-start.16
  195.1 3.2 copy-start.16
  203.0 4.7 copy-start.40
  203.0 4.7 copy-start.41
  204.8 5.7 %slice-start.2 = ((s8[4718592]{0:T(1024)(128)(4,1)}), s8[4194304]{0:T(1024)(128)(4,1)S(1)}, s32[]{:S(2)}) async-start(s8[4718592]{0:T(1024)(128)(4,1)} %bitcast.340), calls=%async_computation.6 | async-start | bytes 8388608
  207.3 14.3 %copy-start.18 = (f32[512,768]{1,0:T(8,128)}, f32[512,768]{1,0:T(8,128)S(1)}, u32[]{:S(2)}) copy-start(f32[512,768]{1,0:T(8,128)S(1)} %get-tuple-element.628) | copy-start | bytes 4718596
  210.5 8.1 %copy-start.72 = (f32[512,3072]{1,0:T(8,128)}, f32[512,3072]{1,0:T(8,128)S(1)}, u32[]{:S(2)}) copy-start(f32[512,3072]{1,0:T(8,128)S(1)} %fusion.75) | copy-start | bytes 18874372
  228.4 3.9 copy-start.4
  228.4 3.9 copy-start.9
  241.3 8.4 %copy-start.2 = (bf16[1,512,768]{1,2,0:T(8,128)(2,1)S(1)}, bf16[1,512,768]{1,2,0:T(8,128)(2,1)}, u32[]{:S(2)}) copy-start(bf16[1,512,768]{1,2,0:T(8,128)(2,1)} %copy-done.1) | copy-start | bytes 2359300 | tf_op jit(solution)/shard_map/while
  241.3 8.4 %copy-start.6 = (f32[1,512,12,64]{1,3,2,0:T(8,128)S(1)}, f32[1,512,12,64]{1,3,2,0:T(8,128)}, u32[]{:S(2)}) copy-start(f32[1,512,12,64]{1,3,2,0:T(8,128)} %get-tuple-element.835) | copy-start | bytes 4718596 | tf_op jit(solution)/shard_map/while
  249.7 4.6 copy-start.3
  249.7 4.8 copy-start.5
  259.0 3.9 copy-start.4
  259.0 3.9 copy-start.9
  271.9 8.4 %copy-start.2 = (bf16[1,512,768]{1,2,0:T(8,128)(2,1)S(1)}, bf16[1,512,768]{1,2,0:T(8,128)(2,1)}, u32[]{:S(2)}) copy-start(bf16[1,512,768]{1,2,0:T(8,128)(2,1)} %copy-done.1) | copy-start | bytes 2359300 | tf_op jit(solution)/shard_map/while
  271.9 8.4 %copy-start.6 = (f32[1,512,12,64]{1,3,2,0:T(8,128)S(1)}, f32[1,512,12,64]{1,3,2,0:T(8,128)}, u32[]{:S(2)}) copy-start(f32[1,512,12,64]{1,3,2,0:T(8,128)} %get-tuple-element.835) | copy-start | bytes 4718596 | tf_op jit(solution)/shard_map/while
  280.3 4.6 copy-start.3
  280.3 4.8 copy-start.5
  289.6 4.6 copy-start.19
  289.6 4.6 copy-start.67
  310.5 5.6 %copy-start.8 = (f32[1,512,12,64]{1,3,2,0:T(8,128)S(1)}, f32[1,512,12,64]{1,3,2,0:T(8,128)}, u32[]{:S(2)}) copy-start(f32[1,512,12,64]{1,3,2,0:T(8,128)} %get-tuple-element.395) | copy-start | bytes 4718596
  310.6 6.6 %copy-start.13 = (f32[512,768]{1,0:T(8,128)S(1)}, f32[512,768]{1,0:T(8,128)}, u32[]{:S(2)}) copy-start(f32[512,768]{1,0:T(8,128)} %copy-done.12) | copy-start | bytes 4718596
  310.6 6.6 %copy-start.25 = (bf16[1,512,12,64]{1,3,2,0:T(8,128)(2,1)S(1)}, bf16[1,512,12,64]{1,3,2,0:T(8,128)(2,1)}, u32[]{:S(2)}) copy-start(bf16[1,512,12,64]{1,3,2,0:T(8,128)(2,1)} %copy-done.24) | copy-start | bytes 2359300
  317.1 10.0 %slice-start.4 = ((s8[4718592]{0:T(1024)(128)(4,1)}), s8[4194304]{0:T(1024)(128)(4,1)S(1)}, s32[]{:S(2)}) async-start(s8[4718592]{0:T(1024)(128)(4,1)} %bitcast.343), calls=%async_computation.8 | async-start | bytes 8388608
  317.1 10.0 %slice-start.8 = ((s8[6291456]{0:T(1024)(128)(4,1)}), s8[4194304]{0:T(1024)(128)(4,1)S(1)}, s32[]{:S(2)}) async-start(s8[6291456]{0:T(1024)(128)(4,1)} %bitcast.400), calls=%async_computation.12 | async-start | bytes 8388608
  318.0 9.2 %copy-start.20 = (f32[512,768]{1,0:T(8,128)S(1)}, f32[512,768]{1,0:T(8,128)}, u32[]{:S(2)}) copy-start(f32[512,768]{1,0:T(8,128)} %copy-done.18) | copy-start | bytes 4718596
  318.0 9.2 %slice-start.5 = ((s8[4718592]{0:T(1024)(128)(4,1)}), s8[524288]{0:T(1024)(128)(4,1)S(1)}, s32[]{:S(2)}) async-start(s8[4718592]{0:T(1024)(128)(4,1)} %bitcast.343), calls=%async_computation.9 | async-start | bytes 1048576
  318.0 9.2 %copy-start.68 = (f32[768]{0:T(1024)S(1)}, f32[768]{0:T(1024)}, u32[]{:S(2)}) copy-start(f32[768]{0:T(1024)} %reshape.715) | copy-start | bytes 9220
  318.0 9.2 %slice-start.9 = ((s8[6291456]{0:T(1024)(128)(4,1)}), s8[2097152]{0:T(1024)(128)(4,1)S(1)}, s32[]{:S(2)}) async-start(s8[6291456]{0:T(1024)(128)(4,1)} %bitcast.400), calls=%async_computation.13 | async-start | bytes 4194304
  327.2 4.9 copy-start.15
  327.2 4.9 copy-start.54
  327.2 4.9 copy-start.57
  332.1 7.0 %copy-start.29 = (bf16[1,512,12,64]{1,3,2,0:T(8,128)(2,1)S(1)}, bf16[1,512,12,64]{1,3,2,0:T(8,128)(2,1)}, u32[]{:S(2)}) copy-start(bf16[1,512,12,64]{1,3,2,0:T(8,128)(2,1)} %convert.67) | copy-start | bytes 2359300
  332.1 7.0 %copy-start.34 = (bf16[1,1,512,1536]{2,3,1,0:T(8,128)(2,1)S(1)}, bf16[1,1,512,1536]{2,3,1,0:T(8,128)(2,1)}, u32[]{:S(2)}) copy-start(bf16[1,1,512,1536]{2,3,1,0:T(8,128)(2,1)} %reduce-scatter.2.cloned.1.call-done) | copy-start | bytes 4718596
  332.1 8.0 %copy-start.61 = (f32[512]{0:T(512)S(1)}, f32[512]{0:T(512)}, u32[]{:S(2)}) copy-start(f32[512]{0:T(512)} %copy-done.60) | copy-start | bytes 6148
  332.1 8.0 %copy-start.65 = (f32[768]{0:T(1024)S(1)}, f32[768]{0:T(1024)}, u32[]{:S(2)}) copy-start(f32[768]{0:T(1024)} %copy-done.64) | copy-start | bytes 9220
  366.0 3.9 slice-start
  366.0 4.0 slice-start.1
  369.2 3.4 slice-start.6
  505.3 4.4 copy-start.70
  505.3 5.0 copy-start.69
  511.6 4.9 copy-start.33
  511.6 4.9 copy-start.62
  511.6 4.9 copy-start.63
  516.5 3.7 copy-start.42
  516.5 3.6 copy-start.43
  516.5 3.6 copy-start.44
  516.5 3.6 copy-start.45
  (38 other events, 79.2 us)
Sparse Core Ops, SparseCore 0:
  154.0 9.9 all-gather.6
  166.1 10.9 all-gather.4
  289.8 12.0 reduce-scatter.1

commit v3 on v1

--- a/solution.py
+++ b/solution.py
@@ -3,6 +3,8 @@
 import jax
 import jax.numpy as jnp
 from jax import lax
+from jax.experimental import pallas as pl
+from jax.experimental.pallas import tpu as pltpu
 from jax.sharding import PartitionSpec as P
 
 HEADS = 12
@@ -84,6 +86,301 @@
         return (new_max, row_total, weighted)
 
     return lax.fori_loop(0, block_count, one_block, state_now)
+
+
+TILE = 16
+MESH_ID = pl.DeviceIdType.MESH
+
+
+def peer_table():
+    dp, z, core = lax.axis_index("dp"), lax.axis_index("fsdp"), lax.axis_index("ctx")
+    row, col = dp // 2, dp % 2
+    sibling = {"ctx": 1 - core}
+    beside = {"dp": row * 2 + (1 - col)}
+    above = {"dp": (1 - row) * 2 + col}
+    across = {"dp": (1 - row) * 2 + (1 - col)}
+    return row, col, z, core, sibling, beside, above, across
+
+
+def greet(peers):
+    barrier = pltpu.get_barrier_semaphore()
+    for peer in peers:
+        pl.semaphore_signal(barrier, inc=1, device_id=peer, device_id_type=MESH_ID)
+    pl.semaphore_wait(barrier, len(peers))
+
+
+def push(source, target, sems, slot, peer):
+    return pltpu.make_async_remote_copy(
+        src_ref=source,
+        dst_ref=target,
+        send_sem=sems.at[0, slot],
+        recv_sem=sems.at[1, slot],
+        device_id=peer,
+        device_id_type=MESH_ID,
+    )
+
+
+def half_of(ref, core):
+    width = ref.shape[-1] // 2
+    return pl.ds(pl.multiple_of(core * width, 128), width)
+
+
+def gather_kernel(count, *refs):
+    owns, wholes = refs[:count], refs[count : 2 * count]
+    line_sems, plane_sems, pair_sems, keep_sems = refs[2 * count :]
+    row, col, z, core, sibling, beside, above, across = peer_table()
+    line_peers = [{"fsdp": lax.rem(z + 4 - k, 4)} for k in (1, 2, 3)]
+    greet([sibling, beside, above, across] + line_peers)
+    line = []
+    for m, (own, whole) in enumerate(zip(owns, wholes)):
+        half = half_of(own, core)
+        for k in (0, 2, 1):
+            line.append(
+                push(
+                    own.at[row, col, :, half],
+                    whole.at[z, row, col, :, half],
+                    line_sems,
+                    m * 3 + k,
+                    line_peers[k],
+                )
+            )
+            line[-1].start()
+    keeps = []
+    for m, (own, whole) in enumerate(zip(owns, wholes)):
+        keeps.append(pltpu.make_async_copy(own, whole.at[z], keep_sems.at[m]))
+        keeps[-1].start()
+    origins = [lax.rem(z + 1 + k, 4) for k in (0, 2, 1)]
+    plane = []
+    for m, whole in enumerate(wholes):
+        half = half_of(whole, core)
+        for step, origin in enumerate(origins):
+            slot = m * 3 + step
+            line[slot].wait_recv()
+            piece = whole.at[origin, row, col, :, half]
+            plane.append(
+                [
+                    push(piece, piece, plane_sems, slot * 3 + index, peer)
+                    for index, peer in enumerate((beside, above, across))
+                ]
+            )
+            for copy in plane[-1]:
+                copy.start()
+    pair = []
+    for m, whole in enumerate(wholes):
+        half = half_of(whole, core)
+        for step, origin in enumerate(origins):
+            slot = m * 3 + step
+            for copy in plane[slot]:
+                copy.wait_recv()
+            piece = whole.at[origin, :, :, :, half]
+            pair.append(push(piece, piece, pair_sems, slot, sibling))
+            pair[-1].start()
+    for copy in pair:
+        copy.wait()
+    for copies in plane:
+        for copy in copies:
+            copy.wait_send()
+    for copy in line:
+        copy.wait_send()
+    for copy in keeps:
+        copy.wait()
+
+
+def gather_all(owns):
+    count = len(owns)
+    return pl.pallas_call(
+        lambda *refs: gather_kernel(count, *refs),
+        out_shape=tuple(jax.ShapeDtypeStruct((4,) + own.shape, own.dtype) for own in owns),
+        in_specs=[pl.BlockSpec(memory_space=pl.ANY)] * count,
+        out_specs=tuple([pl.BlockSpec(memory_space=pl.ANY)] * count),
+        scratch_shapes=[
+            pltpu.SemaphoreType.DMA((2, 3 * count)),
+            pltpu.SemaphoreType.DMA((2, 9 * count)),
+            pltpu.SemaphoreType.DMA((2, 3 * count)),
+            pltpu.SemaphoreType.DMA((count,)),
+        ],
+        compiler_params=pltpu.CompilerParams(collective_id=1, has_side_effects=True),
+        name="gather_weights",
+    )(*owns)
+
+
+def add_rows(pairs, start, rows):
+    @pl.loop(0, 4)
+    def _(shard):
+        @pl.loop(0, rows // TILE)
+        def _(step):
+            offset = pl.multiple_of(step * TILE, TILE)
+            for target, target_at, source, source_at in pairs:
+                here = (shard,) + target_at + (pl.ds(start + offset, TILE),)
+                there = (shard,) + source_at + (pl.ds(offset, TILE),)
+                target[here] = (
+                    target[here].astype(jnp.float32) + source[there].astype(jnp.float32)
+                ).astype(target.dtype)
+
+
+def first_cut(rows, width):
+    return TILE if width >= 3072 else (rows // 2 + TILE - 1) // TILE * TILE
+
+
+def sum_kernel(count, *refs):
+    grads, shared = refs[:count], refs[count : 2 * count]
+    groups = [refs[(2 + i) * count : (3 + i) * count] for i in range(7)]
+    held, from_pair, from_beside, from_above, late_beside, late_above, from_line = groups
+    (
+        load_sems,
+        pair_sems,
+        beside_sems,
+        above_sems,
+        late_beside_sems,
+        late_above_sems,
+        line_sems,
+        plane_sems,
+        last_sems,
+        own_sems,
+    ) = refs[9 * count :]
+    row, col, z, core, sibling, beside, above, across = peer_table()
+    line_peers = [{"fsdp": lax.rem(z + 1 + k, 4)} for k in range(3)]
+    greet([sibling, beside, above, across] + line_peers)
+    loads, pairs = [], []
+    for m in range(count):
+        mine, theirs = half_of(grads[m], core), half_of(grads[m], 1 - core)
+        pairs.append(
+            push(grads[m].at[:, :, :, :, theirs], from_pair[m], pair_sems, m, sibling)
+        )
+        pairs[-1].start()
+        loads.append(
+            pltpu.make_async_copy(grads[m].at[:, :, :, :, mine], held[m], load_sems.at[m])
+        )
+        loads[-1].start()
+    cuts = [first_cut(g.shape[3], g.shape[4]) for g in grads]
+    tails = [g.shape[3] - cut for g, cut in zip(grads, cuts)]
+    corners = [(r, c) for r in range(2) for c in range(2)]
+    first = []
+    for m in range(count):
+        head, rest = pl.ds(0, cuts[m]), pl.ds(cuts[m], tails[m])
+        loads[m].wait()
+        pairs[m].wait_recv()
+        add_rows([(held[m], at, from_pair[m], at) for at in corners], 0, cuts[m] + tails[m])
+        first.append(
+            (
+                push(held[m].at[:, :, 1 - col, head], from_beside[m], beside_sems, m, beside),
+                push(held[m].at[:, 1 - row, :, rest], from_above[m], above_sems, m, above),
+            )
+        )
+        for copy in first[-1]:
+            copy.start()
+    second = []
+    for m in range(count):
+        head, rest = pl.ds(0, cuts[m]), pl.ds(cuts[m], tails[m])
+        for copy in first[m]:
+            copy.wait_recv()
+        add_rows([(held[m], (r, col), from_beside[m], (r,)) for r in range(2)], 0, cuts[m])
+        add_rows([(held[m], (row, c), from_above[m], (c,)) for c in range(2)], cuts[m], tails[m])
+        second.append(
+            (
+                push(
+                    held[m].at[:, 1 - row, col, head], late_above[m], late_above_sems, m, above
+                ),
+                push(
+                    held[m].at[:, row, 1 - col, rest], late_beside[m], late_beside_sems, m, beside
+                ),
+            )
+        )
+        for copy in second[-1]:
+            copy.start()
+    line = []
+    for m in range(count):
+        for copy in second[m]:
+            copy.wait_recv()
+        add_rows([(held[m], (row, col), late_above[m], ())], 0, cuts[m])
+        add_rows([(held[m], (row, col), late_beside[m], ())], cuts[m], tails[m])
+        line.append(
+            [
+                push(
+                    held[m].at[lax.rem(z + 1 + k, 4), row, col],
+                    from_line[m].at[k],
+                    line_sems,
+                    m * 3 + k,
+                    line_peers[k],
+                )
+                for k in range(3)
+            ]
+        )
+        for copy in line[-1]:
+            copy.start()
+    plane, owns = [], []
+    for m in range(count):
+        for copy in line[m]:
+            copy.wait_recv()
+
+        @pl.loop(0, (cuts[m] + tails[m]) // TILE)
+        def _(step):
+            here = pl.ds(pl.multiple_of(step * TILE, TILE), TILE)
+            total = held[m][z, row, col, here].astype(jnp.float32)
+            for k in range(3):
+                total = total + from_line[m][k, here].astype(jnp.float32)
+            held[m][z, row, col, here] = total.astype(held[m].dtype)
+
+        target = shared[m].at[row, col, :, half_of(shared[m], core)]
+        plane.append(
+            [
+                push(held[m].at[z, row, col], target, plane_sems, m * 3 + index, peer)
+                for index, peer in enumerate((beside, above, across))
+            ]
+        )
+        for copy in plane[-1]:
+            copy.start()
+        owns.append(pltpu.make_async_copy(held[m].at[z, row, col], target, own_sems.at[m]))
+        owns[-1].start()
+    last = []
+    for m in range(count):
+        for copy in plane[m]:
+            copy.wait_recv()
+        owns[m].wait()
+        piece = shared[m].at[:, :, :, half_of(shared[m], core)]
+        last.append(push(piece, piece, last_sems, m, sibling))
+        last[-1].start()
+    for copies in first + second + line + plane:
+        for copy in copies:
+            copy.wait_send()
+    for copy in pairs:
+        copy.wait_send()
+    for copy in last:
+        copy.wait()
+
+
+def sum_all(grads):
+    count = len(grads)
+
+    def rooms(shape_of):
+        found = []
+        for g in grads:
+            rows, width = g.shape[-2:]
+            cut = first_cut(rows, width)
+            found.append(pltpu.VMEM(shape_of(rows, cut, rows - cut) + (width // 2,), g.dtype))
+        return found
+
+    return pl.pallas_call(
+        lambda *refs: sum_kernel(count, *refs),
+        out_shape=tuple(jax.ShapeDtypeStruct(g.shape[1:], g.dtype) for g in grads),
+        in_specs=[pl.BlockSpec(memory_space=pl.ANY)] * count,
+        out_specs=tuple([pl.BlockSpec(memory_space=pl.ANY)] * count),
+        scratch_shapes=rooms(lambda rows, cut, tail: (4, 2, 2, rows))
+        + rooms(lambda rows, cut, tail: (4, 2, 2, rows))
+        + rooms(lambda rows, cut, tail: (4, 2, cut))
+        + rooms(lambda rows, cut, tail: (4, 2, tail))
+        + rooms(lambda rows, cut, tail: (4, tail))
+        + rooms(lambda rows, cut, tail: (4, cut))
+        + rooms(lambda rows, cut, tail: (3, rows))
+        + [pltpu.SemaphoreType.DMA((count,))]
+        + [pltpu.SemaphoreType.DMA((2, count))] * 5
+        + [pltpu.SemaphoreType.DMA((2, 3 * count))] * 2
+        + [pltpu.SemaphoreType.DMA((2, count)), pltpu.SemaphoreType.DMA((count,))],
+        compiler_params=pltpu.CompilerParams(
+            collective_id=2, has_side_effects=True, vmem_limit_bytes=48 * 1024 * 1024
+        ),
+        name="sum_gradients",
+    )(*grads)
 
 
 def body(
@@ -131,8 +428,43 @@
             norm2_shift,
         ]
     )
-    small_rows = lax.all_gather(small_row, "fsdp", axis=0, tiled=False)
     part = model_width // shards
+    fits = (lax.axis_size("dp"), shards, lax.axis_size("ctx")) == (4, 4, 2)
+    small_lines = small_row.shape[0] // model_width
+
+    def cut_rows(matrix, groups):
+        return matrix.reshape(groups, 2, 2, -1, matrix.shape[-1])
+
+    def with_small(matrix, small, groups):
+        lines = small.reshape(groups, 1, 1, small_lines, model_width)
+        lines = jnp.pad(lines, ((0, 0), (0, 1), (0, 1), (0, TILE - small_lines), (0, 0)))
+        return jnp.concatenate([cut_rows(matrix, groups), lines], axis=3)
+
+    def split_small(joined):
+        rows = joined.shape[-2] - TILE
+        matrix = joined[..., :rows, :].reshape(-1, model_width)
+        small = joined[..., 0, 0, rows : rows + small_lines, :]
+        return matrix, small.reshape(joined.shape[:-4] + (-1,))
+
+    if fits:
+        whole_qkv, joined, whole_up, whole_down = gather_all(
+            (
+                cut_rows(w_qkv, 1)[0],
+                with_small(w_out, small_row, 1)[0],
+                cut_rows(w_up, 1)[0],
+                cut_rows(w_down, 1)[0],
+            )
+        )
+        whole_out, small_rows = split_small(joined)
+        whole_qkv, whole_up, whole_down = (
+            whole.reshape(-1, whole.shape[-1]) for whole in (whole_qkv, whole_up, whole_down)
+        )
+    else:
+        small_rows = lax.all_gather(small_row, "fsdp", axis=0, tiled=False)
+        whole_qkv = gather_whole(w_qkv)
+        whole_out = gather_whole(w_out)
+        whole_up = gather_whole(w_up)
+        whole_down = gather_whole(w_down)
 
     def small_part(start, width):
         return small_rows[:, start : start + width].reshape(-1)
@@ -147,10 +479,6 @@
     shift_one = small_part(rest + 2 * part, part)
     gain_two = small_part(rest + 3 * part, part)
     shift_two = small_part(rest + 4 * part, part)
-    whole_qkv = gather_whole(w_qkv)
-    whole_out = gather_whole(w_out)
-    whole_up = gather_whole(w_up)
-    whole_down = gather_whole(w_down)
     flat_in = inputs.reshape(row_count, model_width).astype(jnp.float32)
     normed_one, scale_one = normalize(flat_in)
     hidden_one = (normed_one * gain_one.astype(jnp.float32) + shift_one.astype(jnp.float32)).astype(
@@ -375,24 +703,40 @@
         axis=1,
     )
     small_width = small_grads.shape[1]
-    piece_width = small_width // copies
-    out_rows = model_width // (shards * copies)
-    packed = jnp.concatenate(
-        [
-            grad_out.astype(jnp.bfloat16).reshape(shards * copies, out_rows, model_width),
-            jnp.pad(
-                small_grads.astype(jnp.bfloat16).reshape(shards * copies, 1, piece_width),
-                ((0, 0), (0, 7), (0, model_width - piece_width)),
-            ),
-        ],
-        axis=1,
-    )
-    own_down = share(grad_down)
-    own_up = share(grad_up)
-    own_qkv = share(grad_qkv_w)
-    own_packed = share(packed)
-    own_out = own_packed[:, :out_rows].reshape(copies * out_rows, model_width)
-    own_small = own_packed[:, out_rows, :piece_width].reshape(small_width)
+    if fits:
+        up_sum, down_sum, qkv_sum, joined = sum_all(
+            (
+                cut_rows(grad_up.astype(jnp.bfloat16), shards),
+                cut_rows(grad_down.astype(jnp.bfloat16), shards),
+                cut_rows(grad_qkv_w.astype(jnp.bfloat16), shards),
+                with_small(
+                    grad_out.astype(jnp.bfloat16), small_grads.astype(jnp.bfloat16), shards
+                ),
+            )
+        )
+        own_qkv, own_up, own_down = (
+            g.reshape(-1, g.shape[-1]).astype(jnp.float32) for g in (qkv_sum, up_sum, down_sum)
+        )
+        own_out, own_small = (g.astype(jnp.float32) for g in split_small(joined))
+    else:
+        piece_width = small_width // copies
+        out_rows = model_width // (shards * copies)
+        packed = jnp.concatenate(
+            [
+                grad_out.astype(jnp.bfloat16).reshape(shards * copies, out_rows, model_width),
+                jnp.pad(
+                    small_grads.astype(jnp.bfloat16).reshape(shards * copies, 1, piece_width),
+                    ((0, 0), (0, 7), (0, model_width - piece_width)),
+                ),
+            ],
+            axis=1,
+        )
+        own_down = share(grad_down)
+        own_up = share(grad_up)
+        own_qkv = share(grad_qkv_w)
+        own_packed = share(packed)
+        own_out = own_packed[:, :out_rows].reshape(copies * out_rows, model_width)
+        own_small = own_packed[:, out_rows, :piece_width].reshape(small_width)
 
     def own_part(start, width):
         return own_small[start : start + width]

time: 829 us -> 452 us (0.55)
  waiting for transfers between devices: 559 us -> 15.7 us
  Pallas kernels: 0 us -> 224 us
  blocking collectives: 35.8 us -> 0 us
  matrix products: 128 us -> 113 us
    reduce_scatter x4 -> x0, waiting for transfers between devices: 322 us -> none  [share(): lax.psum_scatter(grad.astype(jnp.bfloat16), spread, scatter_dimension=0,...]
    pallas_call x0 -> x2, Pallas kernels: none -> 224 us  [the longest x1 115 us: gather_all(): pl.pallas_call(lambda *refs: gather_kernel(count, *refs), out_shape=tuple...]
    all_gather x6 -> x0, waiting for transfers between devices: 214 us -> none  [the longest x4 193 us: gather_whole(): return lax.all_gather(own_piece(shard), spread, axis=0, tiled=True)]
    all_gather x3 -> x0, blocking collectives: 35.8 us -> none  [the longest x2 25 us: share(): lax.all_gather(piece, ('dp', 'ctx'), axis=0, tiled=True).astype(jnp.float32)]
    reduce_scatter x1, waiting for transfers between devices: 9.42 us -> 0.01 us  [body(): lax.psum_scatter(key_terms.astype(jnp.bfloat16), 'ctx', scatter_dimension...]
  transfers between devices with their start and end apart: 13 -> 3, of which waited for: 12 -> 2; matrix products, arithmetic and copies ran while one was open for 21% -> 7% of each run, Pallas kernels for 0% -> 0%
where the time goes in v3:
time: 452 us; the launch traced here: 447 us
  Pallas kernels  224 us (50%)
  matrix products  113 us (25%)
  local copies, waits for them, and re-layouts  45 us (10%)
  other arithmetic  32.4 us (7%)
  waiting for transfers between devices  15.7 us (3%)
  between operations  14.6 us (3%)
    pallas_call x1, Pallas kernels, gather_all(): pl.pallas_call(lambda *refs: gather_kernel(count, *refs), out_shape=tuple...  115 us
    pallas_call x1, Pallas kernels, sum_all(): pl.pallas_call(lambda *refs: sum_kernel(count, *refs), out_shape=tuple((j...  109 us
    dot_general x2, matrix products, score_grads(): jnp.einsum('sqhd,skhd->sqhk', grad_block, value_block, preferred_element_...  16.7 us
    all_gather x1, waiting for transfers between devices, body(): lax.all_gather(key_rows, 'ctx', axis=1, tiled=True)  11.4 us
    dot_general x2, matrix products, back_block(): jnp.einsum('sqhk,sqhd->skhd', soft_probs.astype(jnp.bfloat16), grad_atten...  10.2 us
    while x66, local copies, waits for them, and re-layouts  9.94 us
  transfers between devices with their start and end apart: 3, of which 2 were waited for; matrix products, arithmetic and copies ran while one was open for 7% of the time, Pallas kernels for 0%

profile of v3, /device:TPU:9, one launch (start us, length us, event | category | flops | bytes accessed | tf_op | source)
XLA Modules:
  0.0 446.9 jit_solution(2568559617242454046)
XLA Ops:
  8.0 1.3 convert_reduce_fusion
  9.3 1.5 fusion.68
  10.8 4.8 %concatenate.23 = bf16[2304]{0:T(1024)(128)(2,1)S(1)} concatenate(bf16[384]{0:T(512)(128)(2,1)S(1)} %reshape.657, bf16[192]{0:T(256)(128)(2,1)} %param.27, bf16[768]{0:T(1024)(128)(2,1)} %param.28, bf16[192]{0:T(256)(128)(2,1)} %param.29, bf16[192]{0:T(256)(128)(2,1)} %param.30, bf16[192]{0:T(256)(128)(2,1)} %param.31, bf16[192]{0:T(256)(128)(2,1)} %param.32, bf16[192]{0:T(256)(128)(2,1)} %param.33), dimensions={0} | concatenate | bytes 9216 | tf_op jit(solution)/shard_map/concatenate | solution.py:419
  15.7 1.7 fusion.98.refs_1_
  17.4 114.7 %gather_weights.1 = (bf16[4,2,2,48,2304]{4,3,2,1,0:T(8,128)(2,1)}, bf16[4,2,2,64,768]{4,3,2,1,0:T(8,128)(2,1)}, bf16[4,2,2,48,3072]{4,3,2,1,0:T(8,128)(2,1)}, bf16[4,2,2,192,768]{4,3,2,1,0:T(8,128)(2,1)}) custom-call(bf16[2,2,48,2304]{3,2,1,0:T(8,128)(2,1)} %bitcast.345, bf16[2,2,64,768]{3,2,1,0:T(8,128)(2,1)} %fusion.98.refs_1_, ...), custom_call_target="tpu_custom_call" | custom-call | tf_op jit(solution)/shard_map/gather_weights/pallas_call | solution.py:191
  134.0 4.2 fusion.79
  138.2 1.4 fusion.75
  139.6 1.0 copy-done.22
  140.7 2.4 slice.180
  143.4 2.4 slice.117
  146.5 4.2 all-gather.7.cloned.1.call-done
  150.7 1.7 copy.58
  152.5 11.4 %all-gather.5.cloned.1.call-done = bf16[1024,768]{1,0:T(8,128)(2,1)} async-done(((bf16[512,768]{1,0:T(8,128)(2,1)}), bf16[1024,768]{1,0:T(8,128)(2,1)}) %all-gather.5.cloned.1.call-update) | async-done | bytes 1572880 | tf_op jit(solution)/shard_map/all_gather | solution.py:514
  163.9 2.6 copy.57
  166.4 23.3 %while.35 = (s32[]{:T(128)}, f32[1,512,12]{1,2,0:T(8,128)S(1)}, f32[1,512,12]{1,2,0:T(8,128)S(1)}, f32[1,512,12,64]{1,3,2,0:T(8,128)}, s32[4]{0:T(128)S(1)}, /*i...) while((s32[]{:T(128)}, f32[1,512,12]{1,2,0:T(8,128)S(1)}, ...), condition=%wide.region_7.8_spmd.clone, body=%wide.region_3.7_spmd.clone.sunk | while | flops 847700480 | bytes 60438800 | solution.py:88
  166.8 1.3 constant_dynamic-slice_fusion.6
  168.1 2.1 fusion.157
  170.2 3.1 fusion.159
  173.4 3.6 bitcast_add_fusion.7
  177.0 1.1 copy-done.18
  178.4 1.3 constant_dynamic-slice_fusion.6
  179.7 2.1 fusion.157
  181.8 3.1 fusion.159
  185.0 3.6 bitcast_add_fusion.7
  188.6 1.1 copy-done.18
  189.7 1.7 fusion.96
  192.8 5.5 %fusion.107 = f32[512,3072]{1,0:T(8,128)S(1)} fusion(bf16[768,3072]{1,0:T(8,128)(2,1)} %bitcast.360, f32[512,768]{1,0:T(8,128)S(1)} %get-tuple-element.628, f32[768]{0:T(1024)S(1)} %reshape.686, f32[768]{0:T(1024)S(1)} %reshape.685, f32[512]{0:T(512)S(1)} %add_rsqrt_fusion, f32[512]{0:T(512)S(1)} %broadcast_multiply_fusion.4), kind=kOutput, calls=%fused_computation.206 | convolution fusion | flops 2417885184 | bytes 12593152 | tf_op jit(solution)/shard_map/dot_general | solution.py:536
  198.4 8.1 %fusion.111 = (bf16[3072]{0:T(1024)(128)(2,1)S(1)}, bf16[512,3072]{1,0:T(8,128)(2,1)S(1)}) fusion(bf16[3072,768]{1,0:T(8,128)(2,1)S(1)} %bitcast.356, bf16[1,512,768]{2,1,0:T(8,128)(2,1)S(1)} %copy-done.30, f32[512,3072]{1,0:T(8,128)S(1)} %fusion.107, f32[3072]{0:T(1024)S(1)} %reshape.687), kind=kOutput, calls=%fused_computation.210 | convolution fusion | flops 2456810496 | bytes 14960640 | tf_op jit(solution)/shard_map/rd,fd->rf/dot_general | solution.py:550
  206.6 3.1 multiply_reduce_fusion
  210.3 1.2 copy-done.11
  211.6 1.7 convolution_convert_fusion.4
  213.3 1.4 copy.59
  214.7 1.7 multiply_reduce_fusion.1
  216.4 61.0 %while.36 = (s32[]{:T(128)}, f32[1,512,12,64]{1,3,2,0:T(8,128)}, bf16[2,1,512,1536]{2,3,1,0:T(8,128)(2,1)}, s32[2]{0:T(128)S(1)}, bf16[1,1024,768]{1,2,0:T(8,128...) while((s32[]{:T(128)}, f32[1,512,12,64]{1,3,2,0:T(8,128)}, ...), condition=%wide.region_15.16_spmd.clone, body=%wide.region_13.15_spmd.clone.sunk | while | flops 2056409600 | bytes 171530928 | solution.py:659
  218.2 2.2 constant_dynamic-slice_fusion.7
  221.3 3.0 fusion.170
  224.2 5.1 %fusion.173 = bf16[12,512,64]{1,2,0:T(8,128)(2,1)} fusion(f32[12,512,512]{2,1,0:T(8,128)S(1)} %fusion.170, f32[512,12]{0,1:T(8,128)S(1)} %bitcast.352, pred[512,512]{0,1:T(8,128)(4,1)S(1)} %broadcast_compare_fusion.5, bf16[1,512,12,64]{1,3,2,0:T(8,128)(2,1)} %copy-done.27), kind=kOutput, calls=%fused_computation.46.clone.1 | convolution fusion | flops 418381824 | bytes 14442496 | tf_op jit(solution)/shard_map/while/body/eval_jaxpr/sqhk,sqhd->skhd/dot_general | solution.py:644
  229.3 8.3 %fusion.172 = bf16[512,12,512]{0,2,1:T(8,128)(2,1)} fusion(f32[12,512,512]{2,1,0:T(8,128)S(1)} %fusion.170, f32[512,12]{0,1:T(8,128)S(1)} %bitcast.351, f32[512,12]{0,1:T(8,128)S(1)} %bitcast.353, pred[512,512]{0,1:T(8,128)(4,1)S(1)} %broadcast_compare_fusion.5, bf16[512,12,64]{0,2,1:T(8,128)(2,1)} %bitcast.319, bf16[1,512,12,64]{1,3,2,0:T(8,128)(2,1)} %copy-done.27), kind=kOutput, calls=%fused_computation.45.clone.1 | convolution fusion | flops 424673280 | bytes 20758528 | tf_op jit(solution)/shard_map/while/body/eval_jaxpr/sqhd,skhd->sqhk/dot_general | solution.py:601
  237.7 4.1 bitcast_add_fusion.8
  242.4 2.0 convolution_multiply_fusion.2
  245.3 1.6 copy-done.24
  248.6 2.2 constant_dynamic-slice_fusion.7
  251.7 3.0 fusion.170
  254.7 5.1 %fusion.173 = bf16[12,512,64]{1,2,0:T(8,128)(2,1)} fusion(f32[12,512,512]{2,1,0:T(8,128)S(1)} %fusion.170, f32[512,12]{0,1:T(8,128)S(1)} %bitcast.352, pred[512,512]{0,1:T(8,128)(4,1)S(1)} %broadcast_compare_fusion.5, bf16[1,512,12,64]{1,3,2,0:T(8,128)(2,1)} %copy-done.27), kind=kOutput, calls=%fused_computation.46.clone.1 | convolution fusion | flops 418381824 | bytes 14442496 | tf_op jit(solution)/shard_map/while/body/eval_jaxpr/sqhk,sqhd->skhd/dot_general | solution.py:644
  259.8 8.3 %fusion.172 = bf16[512,12,512]{0,2,1:T(8,128)(2,1)} fusion(f32[12,512,512]{2,1,0:T(8,128)S(1)} %fusion.170, f32[512,12]{0,1:T(8,128)S(1)} %bitcast.351, f32[512,12]{0,1:T(8,128)S(1)} %bitcast.353, pred[512,512]{0,1:T(8,128)(4,1)S(1)} %broadcast_compare_fusion.5, bf16[512,12,64]{0,2,1:T(8,128)(2,1)} %bitcast.319, bf16[1,512,12,64]{1,3,2,0:T(8,128)(2,1)} %copy-done.27), kind=kOutput, calls=%fused_computation.45.clone.1 | convolution fusion | flops 424673280 | bytes 20758528 | tf_op jit(solution)/shard_map/while/body/eval_jaxpr/sqhd,skhd->sqhk/dot_general | solution.py:601
  268.1 4.1 bitcast_add_fusion.8
  272.9 2.0 convolution_multiply_fusion.2
  275.8 1.6 copy-done.24
  277.4 1.4 reduce.17
  279.3 1.0 convert.60
  280.7 1.8 convolution_convert_fusion.3
  282.6 6.9 %convolution_convert_fusion.2 = bf16[768,3072]{1,0:T(8,128)(2,1)} fusion(bf16[512,3072]{1,0:T(8,128)(2,1)} %copy-done.51, f32[512,768]{1,0:T(8,128)S(1)} %copy-done.20, f32[768]{0:T(1024)S(1)} %copy-done.49, f32[768]{0:T(1024)S(1)} %reshape.685, f32[512]{0:T(512)S(1)} %add_rsqrt_fusion, f32[512]{0:T(512)S(1)} %broadcast_multiply_fusion.4), kind=kOutput, calls=%fused_computation.93 | convolution fusion | flops 2420244480 | bytes 9447424 | tf_op jit(solution)/shard_map/rd,rf->df/dot_general | solution.py:553
  289.5 8.9 %convolution_convert_fusion.1 = bf16[3072,768]{1,0:T(8,128)(2,1)} fusion(bf16[1,512,768]{2,1,0:T(8,128)(2,1)S(1)} %copy-done.31, f32[512,3072]{1,0:T(8,128)} %copy-done.50, f32[3072]{0:T(1024)S(1)} %reshape.687), kind=kOutput, calls=%fused_computation.92 | convolution fusion | flops 2434007040 | bytes 11808768 | tf_op jit(solution)/shard_map/rf,rd->fd/dot_general | solution.py:548
  298.5 4.9 %fusion.77 = bf16[1,512,768]{2,1,0:T(8,128)(2,1)} fusion(f32[512,768]{1,0:T(8,128)S(1)} %copy-done.20, bf16[3072,768]{1,0:T(8,128)(2,1)S(1)} %bitcast.359, f32[768]{0:T(1024)S(1)} %reshape.688, f32[512,3072]{1,0:T(8,128)S(1)} %bitcast.367, f32[3072]{0:T(1024)S(1)} %reshape.687), kind=kOutput, calls=%fused_computation.140 | convolution fusion | flops 2432827392 | bytes 13384704 | tf_op jit(solution)/shard_map/dot_general | solution.py:542
  303.4 6.7 %fusion.67 = (bf16[768]{0:T(1024)(128)(2,1)S(1)}, f32[512]{0:T(512)}, f32[512]{0:T(512)}, bf16[768]{0:T(1024)(128)(2,1)S(1)}, f32[512,768]{1,0:T(8,128)}) fusion(bf16[1,512,768]{2,1,0:T(8,128)(2,1)S(1)} %copy-done.15, f32[512]{0:T(512)S(1)} %copy-done.43, f32[512]{0:T(512)S(1)} %copy-done.37, f32[768]{0:T(1024)S(1)} %copy-done.40, ...), kind=kOutput, calls=%fused_computation.115 | convolution fusion | flops 1820587520 | bytes 8271872 | tf_op jit(solution)/shard_map/re,de->rd/dot_general | solution.py:672
  310.8 4.3 convolution_convert_fusion
  315.8 109.0 %sum_gradients.1 = (bf16[2,2,48,3072]{3,2,1,0:T(8,128)(2,1)S(1)}, bf16[2,2,192,768]{3,2,1,0:T(8,128)(2,1)S(1)}, bf16[2,2,48,2304]{3,2,1,0:T(8,128)(2,1)S(1)}, bf16[2,2,64,768]{3,2,1,0:T(8,128)(2,1)S(1)}) custom-call(bf16[4,2,2,48,3072]{4,3,2,1,0:T(8,128)(2,1)} %bitcast.323, bf16[4,2,2,192,768]{4,3,2,1,0:T(8,128)(2,1)} %bitcast.324, ...), custom_call_target="tpu_custom_call" | custom-call | tf_op jit(solution)/shard_map/sum_gradients/pallas_call | solution.py:363
  426.1 1.4 slice.154
  427.4 1.5 fusion.108
  429.6 1.3 broadcast_multiply_fusion.1
  433.1 1.4 bitcast_convert_fusion.2
  434.5 1.7 bitcast_convert_fusion.1
  436.2 1.7 bitcast_convert_fusion
  438.7 1.4 fusion.82
  (240 shorter events, 20.6 us)
Async XLA Ops:
  7.2 143.6 %all-gather.7.cloned.1.call-start = ((), (), s32[]{:S(2)}) async-start(), calls=%async_computation.3 | async-start | bytes 2359296 | tf_op jit(solution)/shard_map/all_gather | solution.py:515
  9.3 124.7 %copy-start.36 = (f32[512]{0:T(512)}, f32[512]{0:T(512)S(1)}, u32[]{:S(2)}) copy-start(f32[512]{0:T(512)S(1)} %broadcast_multiply_fusion.5) | copy-start | bytes 6148
  10.8 123.2 %copy-start.14 = (bf16[1,512,768]{2,1,0:T(8,128)(2,1)S(1)}, bf16[1,512,768]{2,1,0:T(8,128)(2,1)}, u32[]{:S(2)}) copy-start(bf16[1,512,768]{2,1,0:T(8,128)(2,1)} %param.19) | copy-start | bytes 2359300
  10.8 127.4 %copy-start.42 = (f32[512]{0:T(512)}, f32[512]{0:T(512)S(1)}, u32[]{:S(2)}) copy-start(f32[512]{0:T(512)S(1)} %add_rsqrt_fusion.1) | copy-start | bytes 6148
  134.0 4.3 copy-start.39
  134.0 4.2 copy-start.46
  138.2 2.4 copy-start.22
  140.6 23.2 %all-gather.5.cloned.1.call-start = ((), (), s32[]{:S(2)}) async-start(), calls=%async_computation.2 | async-start | bytes 2359296 | tf_op jit(solution)/shard_map/all_gather | solution.py:514
  143.1 3.3 copy-start.35
  143.1 160.3 %reduce-scatter.2.cloned.1.call-start = ((), (), s32[]{:S(2)}) async-start(), calls=%async_computation.1 | async-start | bytes 4718592 | tf_op jit(solution)/shard_map/reduce_scatter | solution.py:662
  146.0 46.8 %copy-start.48 = (f32[768]{0:T(1024)}, f32[768]{0:T(1024)S(1)}, u32[]{:S(2)}) copy-start(f32[768]{0:T(1024)S(1)} %reshape.686) | copy-start | bytes 9220
  170.2 3.2 copy-start.17
  181.8 3.2 copy-start.17
  191.5 6.9 %slice-start = ((s8[4718592]{0:T(1024)(128)(4,1)}), s8[4194304]{0:T(1024)(128)(4,1)S(1)}, s32[]{:S(2)}) async-start(s8[4718592]{0:T(1024)(128)(4,1)} %bitcast.354), calls=%async_computation.4 | async-start | bytes 8388608
  192.4 17.2 %copy-start.19 = (f32[512,768]{1,0:T(8,128)}, f32[512,768]{1,0:T(8,128)S(1)}, u32[]{:S(2)}) copy-start(f32[512,768]{1,0:T(8,128)S(1)} %get-tuple-element.628) | copy-start | bytes 4718596
  192.8 5.6 %copy-start.30 = (bf16[1,512,768]{2,1,0:T(8,128)(2,1)S(1)}, bf16[1,512,768]{2,1,0:T(8,128)(2,1)}, u32[]{:S(2)}) copy-start(bf16[1,512,768]{2,1,0:T(8,128)(2,1)} %param.20) | copy-start | bytes 2359300
  192.8 5.6 %slice-start.1 = ((s8[4718592]{0:T(1024)(128)(4,1)}), s8[524288]{0:T(1024)(128)(4,1)S(1)}, s32[]{:S(2)}) async-start(s8[4718592]{0:T(1024)(128)(4,1)} %bitcast.354), calls=%async_computation.5 | async-start | bytes 1048576
  192.8 13.7 %slice-start.4 = ((s8[4718592]{0:T(1024)(128)(4,1)}), s8[4194304]{0:T(1024)(128)(4,1)S(1)}, s32[]{:S(2)}) async-start(s8[4718592]{0:T(1024)(128)(4,1)} %bitcast.361), calls=%async_computation.8 | async-start | bytes 8388608
  198.4 8.1 %copy-start.50 = (f32[512,3072]{1,0:T(8,128)}, f32[512,3072]{1,0:T(8,128)S(1)}, u32[]{:S(2)}) copy-start(f32[512,3072]{1,0:T(8,128)S(1)} %fusion.107) | copy-start | bytes 18874372
  198.4 8.1 %slice-start.5 = ((s8[4718592]{0:T(1024)(128)(4,1)}), s8[524288]{0:T(1024)(128)(4,1)S(1)}, s32[]{:S(2)}) async-start(s8[4718592]{0:T(1024)(128)(4,1)} %bitcast.361), calls=%async_computation.9 | async-start | bytes 1048576
  206.5 3.1 copy-start.51
  216.4 3.9 copy-start.3
  216.4 3.9 copy-start.8
  229.3 8.3 %copy-start.1 = (bf16[1,512,768]{1,2,0:T(8,128)(2,1)S(1)}, bf16[1,512,768]{1,2,0:T(8,128)(2,1)}, u32[]{:S(2)}) copy-start(bf16[1,512,768]{1,2,0:T(8,128)(2,1)} %copy-done) | copy-start | bytes 2359300 | tf_op jit(solution)/shard_map/while
  229.3 8.3 %copy-start.5 = (f32[1,512,12,64]{1,3,2,0:T(8,128)S(1)}, f32[1,512,12,64]{1,3,2,0:T(8,128)}, u32[]{:S(2)}) copy-start(f32[1,512,12,64]{1,3,2,0:T(8,128)} %get-tuple-element.835) | copy-start | bytes 4718596 | tf_op jit(solution)/shard_map/while
  237.7 4.6 %copy-start.2 = (bf16[512,12,512]{0,2,1:T(8,128)(2,1)S(1)}, bf16[512,12,512]{0,2,1:T(8,128)(2,1)}, u32[]{:S(2)}) copy-start(bf16[512,12,512]{0,2,1:T(8,128)(2,1)} %fusion.172) | copy-start | bytes 18874372 | tf_op jit(solution)/shard_map/while
  237.7 4.8 %copy-start.4 = (bf16[1,512,12,64]{1,3,2,0:T(8,128)(2,1)S(1)}, bf16[1,512,12,64]{1,3,2,0:T(8,128)(2,1)}, u32[]{:S(2)}) copy-start(bf16[1,512,12,64]{1,3,2,0:T(8,128)(2,1)} %copy-done.3) | copy-start | bytes 2359300 | tf_op jit(solution)/shard_map/while
  242.4 2.0 copy-start.6
  242.4 2.0 copy-start.10
  242.4 2.7 copy-start.23
  244.4 2.5 copy-start.9
  244.4 2.5 copy-start.28
  246.9 3.9 copy-start.3
  246.9 3.9 copy-start.8
  259.8 8.3 %copy-start.1 = (bf16[1,512,768]{1,2,0:T(8,128)(2,1)S(1)}, bf16[1,512,768]{1,2,0:T(8,128)(2,1)}, u32[]{:S(2)}) copy-start(bf16[1,512,768]{1,2,0:T(8,128)(2,1)} %copy-done) | copy-start | bytes 2359300 | tf_op jit(solution)/shard_map/while
  259.8 8.3 %copy-start.5 = (f32[1,512,12,64]{1,3,2,0:T(8,128)S(1)}, f32[1,512,12,64]{1,3,2,0:T(8,128)}, u32[]{:S(2)}) copy-start(f32[1,512,12,64]{1,3,2,0:T(8,128)} %get-tuple-element.835) | copy-start | bytes 4718596 | tf_op jit(solution)/shard_map/while
  268.1 4.6 %copy-start.2 = (bf16[512,12,512]{0,2,1:T(8,128)(2,1)S(1)}, bf16[512,12,512]{0,2,1:T(8,128)(2,1)}, u32[]{:S(2)}) copy-start(bf16[512,12,512]{0,2,1:T(8,128)(2,1)} %fusion.172) | copy-start | bytes 18874372 | tf_op jit(solution)/shard_map/while
  268.1 4.8 %copy-start.4 = (bf16[1,512,12,64]{1,3,2,0:T(8,128)(2,1)S(1)}, bf16[1,512,12,64]{1,3,2,0:T(8,128)(2,1)}, u32[]{:S(2)}) copy-start(bf16[1,512,12,64]{1,3,2,0:T(8,128)(2,1)} %copy-done.3) | copy-start | bytes 2359300 | tf_op jit(solution)/shard_map/while
  272.9 2.0 copy-start.6
  272.9 2.0 copy-start.10
  272.9 2.7 copy-start.23
  274.9 2.5 copy-start.9
  274.9 2.5 copy-start.28
  277.4 1.9 copy-start.7
  277.4 2.9 copy-start.12
  280.7 1.8 copy-start.49
  282.6 6.9 %copy-start.31 = (bf16[1,512,768]{2,1,0:T(8,128)(2,1)S(1)}, bf16[1,512,768]{2,1,0:T(8,128)(2,1)}, u32[]{:S(2)}) copy-start(bf16[1,512,768]{2,1,0:T(8,128)(2,1)} %param.20) | copy-start | bytes 2359300
  282.6 15.8 %slice-start.2 = ((s8[4718592]{0:T(1024)(128)(4,1)}), s8[4194304]{0:T(1024)(128)(4,1)S(1)}, s32[]{:S(2)}) async-start(s8[4718592]{0:T(1024)(128)(4,1)} %bitcast.357), calls=%async_computation.6 | async-start | bytes 8388608
  282.6 15.8 %slice-start.6 = ((s8[6291456]{0:T(1024)(128)(4,1)}), s8[4194304]{0:T(1024)(128)(4,1)S(1)}, s32[]{:S(2)}) async-start(s8[6291456]{0:T(1024)(128)(4,1)} %bitcast.366), calls=%async_computation.10 | async-start | bytes 8388608
  289.5 8.9 %slice-start.3 = ((s8[4718592]{0:T(1024)(128)(4,1)}), s8[524288]{0:T(1024)(128)(4,1)S(1)}, s32[]{:S(2)}) async-start(s8[4718592]{0:T(1024)(128)(4,1)} %bitcast.357), calls=%async_computation.7 | async-start | bytes 1048576
  289.5 8.9 %slice-start.7 = ((s8[6291456]{0:T(1024)(128)(4,1)}), s8[2097152]{0:T(1024)(128)(4,1)S(1)}, s32[]{:S(2)}) async-start(s8[6291456]{0:T(1024)(128)(4,1)} %bitcast.366), calls=%async_computation.11 | async-start | bytes 4194304
  298.4 4.9 %copy-start.15 = (bf16[1,512,768]{2,1,0:T(8,128)(2,1)S(1)}, bf16[1,512,768]{2,1,0:T(8,128)(2,1)}, u32[]{:S(2)}) copy-start(bf16[1,512,768]{2,1,0:T(8,128)(2,1)} %param.19) | copy-start | bytes 2359300
  298.4 4.9 %copy-start.29 = (bf16[1,512,12,64]{1,3,2,0:T(8,128)(2,1)S(1)}, bf16[1,512,12,64]{1,3,2,0:T(8,128)(2,1)}, u32[]{:S(2)}) copy-start(bf16[1,512,12,64]{1,3,2,0:T(8,128)(2,1)} %convert.60) | copy-start | bytes 2359300
  298.4 4.9 %copy-start.37 = (f32[512]{0:T(512)S(1)}, f32[512]{0:T(512)}, u32[]{:S(2)}) copy-start(f32[512]{0:T(512)} %copy-done.36) | copy-start | bytes 6148
  298.4 4.9 %copy-start.40 = (f32[768]{0:T(1024)S(1)}, f32[768]{0:T(1024)}, u32[]{:S(2)}) copy-start(f32[768]{0:T(1024)} %copy-done.39) | copy-start | bytes 9220
  298.4 4.9 %copy-start.43 = (f32[512]{0:T(512)S(1)}, f32[512]{0:T(512)}, u32[]{:S(2)}) copy-start(f32[512]{0:T(512)} %copy-done.42) | copy-start | bytes 6148
  303.4 6.7 %copy-start.33 = (bf16[1,1,512,1536]{2,3,1,0:T(8,128)(2,1)S(1)}, bf16[1,1,512,1536]{2,3,1,0:T(8,128)(2,1)}, u32[]{:S(2)}) copy-start(bf16[1,1,512,1536]{2,3,1,0:T(8,128)(2,1)} %reduce-scatter.2.cloned.1.call-done) | copy-start | bytes 4718596
  310.8 4.8 %copy-start.21 = (bf16[768,768]{1,0:T(8,128)(2,1)S(1)}, bf16[768,768]{1,0:T(8,128)(2,1)}, u32[]{:S(2)}) copy-start(bf16[768,768]{1,0:T(8,128)(2,1)} %convolution_convert_fusion.3) | copy-start | bytes 3538948
  434.5 3.4 copy-start.32
  436.2 1.9 copy-start.13
  436.2 2.5 copy-start.16
  436.2 2.5 copy-start.41
  436.2 2.5 copy-start.44
  436.2 2.5 copy-start.45
  (15 other events, 19.9 us)
Sparse Core Ops, SparseCore 0:
  140.8 9.9 all-gather.6
  152.9 10.9 all-gather.4
  277.5 12.0 reduce-scatter.1
